TPU v7x, 32 devices: a whole 2x2x4 slice. The times are simulated.
32 devices in a mesh: inst: 8 (over y, x, core), tp: 4 (over z).
Axes of the slice: x: 2, y: 2, z: 4, core: 2. Of those that a mesh axis runs over, the one named last changes fastest.
Arguments:
- fresh_segment_probes: bfloat16 [2048, 64, 128], P('inst', 'tp'), may hold values from -10 to 10
- fresh_segment_pairs: bfloat16 [2048, 2, 8, 128], P('inst', None, 'tp'), may hold values from -5 to 5
- earlier_stored_pairs: bfloat16 [8192, 2, 8, 128], P('inst', None, 'tp'), may hold values from -5 to 5
- emitted_token_probe: bfloat16 [64, 128], P('tp'), may hold values from -10 to 10
- emitted_token_pair: bfloat16 [2, 8, 128], P(None, 'tp'), may hold values from -5 to 5
- final_projection_weights: bfloat16 [8192, 8192], P('tp', 'inst'), may hold values from -0.0625 to 0.0625
- remaining_instance_ids: int32 [4], replicated, may hold values from 0 to 7, as said below
- segment_destination_member: int32 [16, 1], replicated, may hold values from 0 to 3; in each aligned block of 16 rows (0 to 15, 16 to 31, ...) at most 8 rows name the same one
Outputs:
- span_hidden: bfloat16 [2048, 8192], P('inst', 'tp')
- migrated_cache: bfloat16 [8, 1024, 2, 8, 128], P('inst', None, None, 'tp')
- decode_attention: bfloat16 [64, 128], P('tp')
Inputs may be any that keep to these rules, and one draw needn't show every extreme that they name: `segment_destination_member`: at most 8 blocks name one survivor, a bound that some block reaches. `remaining_instance_ids`: 4 distinct instance indices; instances 0 and 7 always survive.
All inputs are finite; a program needn't handle non-finite values.
Results may differ from a plain program's by a relative error of at most 0.024.
Values may be sent and summed in bfloat16 or wider, within the bound.
No kernel may reach another device: no remote copies, remote signals or barrier semaphores. Data moves between devices by JAX's collectives and lax.ppermute only.
A program may use at most 128 MiB of HBM per device.

v0:
```python
import functools

import jax
import jax.numpy as jnp
from jax import lax
from jax.experimental import pallas as pl
from jax.experimental.pallas import tpu as pltpu
from jax.sharding import PartitionSpec as P

BLK = 128
CAP = 8
NEG_FILL = -1e30
LOG2E = 1.4426950408889634
LARGEST = 2.0**100
CHUNKS = 4
GROUP = 2


def from_behind(block, axis, distance):
    devices = range(lax.axis_size(axis))
    route = [((i - distance) % len(devices), i) for i in devices]
    return lax.ppermute(block, axis, route)


def combined_all(value, axis, combine):
    everything = jax.tree.map(lambda part: lax.all_gather(part, axis), value)
    initial = jax.tree.map(lambda part: part[0], everything)

    def turn(k, so_far):
        return combine(so_far, jax.tree.map(lambda part: part[k], everything))

    return lax.fori_loop(1, lax.axis_size(axis), turn, initial)


def attend(state, queries, key_value, visible):
    width = queries.shape[-1]
    scores = jnp.einsum(
        "rkgd,nkd->rkgn", queries, key_value[:, 0], preferred_element_type=jnp.float32
    ) * width ** (-0.5)
    if visible is not None:
        scores = jnp.where(visible[:, None, None, :], scores, NEG_FILL)
    running, total, weighted = state
    highest = jnp.maximum(running, jnp.max(scores, axis=-1))
    factor = jnp.exp(running - highest)
    weights = jnp.exp(scores - highest[..., None])
    total = total * factor + jnp.sum(weights, axis=-1)
    update = jnp.einsum(
        "rkgn,nkd->rkgd",
        weights.astype(jnp.bfloat16),
        key_value[:, 1],
        preferred_element_type=jnp.float32,
    )
    weighted = weighted * factor[..., None] + update
    return (highest, total, weighted)


def empty_state(rows, slots_local, group, width):
    return (
        jnp.full((rows, slots_local, group), -jnp.inf, jnp.float32),
        jnp.zeros((rows, slots_local, group), jnp.float32),
        jnp.zeros((rows, slots_local, group, width), jnp.float32),
    )


def combine(first, second):
    highest = jnp.maximum(first[0], second[0])
    left = jnp.exp(first[0] - highest)
    right = jnp.exp(second[0] - highest)
    return (
        highest,
        first[1] * left + second[1] * right,
        first[2] * left[..., None] + second[2] * right[..., None],
    )


def place_blocks(cache, rows_in, destination_members, slots, own_index):
    count = rows_in.shape[0] // BLK

    def put(index, current):
        spot = slots[index] * BLK
        incoming = lax.dynamic_slice_in_dim(rows_in, index * BLK, BLK, 0)
        present = lax.dynamic_slice_in_dim(current, spot, BLK, 0)
        chosen = jnp.where(destination_members[index] == own_index, incoming, present)
        return lax.dynamic_update_slice_in_dim(current, chosen, spot, 0)

    return lax.fori_loop(0, count, put, cache)


def destinations(segment_destination_member, remaining_instance_ids):
    sequence = segment_destination_member[:, 0]
    agreement = (
        sequence[:, None]
        == jnp.arange(remaining_instance_ids.shape[0], dtype=jnp.int32)[None, :]
    ).astype(jnp.int32)
    slots = jnp.sum(jnp.cumsum(agreement, axis=0) * agreement, axis=1) - 1
    members = jnp.sum(agreement * remaining_instance_ids[None, :], axis=1)
    return slots, members


def on_device_ring(
    fresh_segment_probes,
    fresh_segment_pairs,
    earlier_stored_pairs,
    emitted_token_probe,
    emitted_token_pair,
    final_projection_weights,
    remaining_instance_ids,
    segment_destination_member,
):
    own_index = lax.axis_index("inst")
    instances = lax.axis_size("inst")
    rows, heads, width = fresh_segment_probes.shape
    slots_local = fresh_segment_pairs.shape[2]
    group = heads // slots_local
    queries = fresh_segment_probes.reshape(rows, slots_local, group, width)
    slots, destination_members = destinations(segment_destination_member, remaining_instance_ids)
    held_blocks = jnp.sum((destination_members == own_index).astype(jnp.int32))
    cache = jnp.zeros((CAP * BLK, 2, slots_local, width), jnp.bfloat16)
    causal = jnp.arange(rows)[:, None] >= jnp.arange(rows)[None, :]
    state = attend(
        empty_state(rows, slots_local, group, width), queries, earlier_stored_pairs, None
    )
    state = attend(state, queries, fresh_segment_pairs, causal)
    moving = jnp.concatenate([fresh_segment_pairs, earlier_stored_pairs], axis=0)

    def turn_both(step, carry):
        moving, state, current = carry
        moving = from_behind(moving, "inst", 1)
        source = (own_index - step) % instances
        state = attend(state, queries, moving[rows:], None)
        visible = jnp.broadcast_to(source < own_index, (rows, rows))
        state = attend(state, queries, moving[:rows], visible)
        return (moving, state, current)

    moving, state, cache = lax.fori_loop(1, instances, turn_both, (moving, state, cache))
    cache = place_blocks(
        cache,
        lax.all_gather(fresh_segment_pairs, "inst", axis=0, tiled=True),
        destination_members,
        slots,
        own_index,
    )
    attention = (state[2] / state[1][..., None]).astype(jnp.bfloat16).reshape(rows, heads * width)
    terms = jnp.dot(
        attention,
        lax.all_gather(final_projection_weights, "inst", axis=1, tiled=True),
        preferred_element_type=jnp.float32,
    )
    span_hidden = lax.psum_scatter(
        terms.astype(jnp.bfloat16), "tp", scatter_dimension=1, tiled=True
    )
    single = emitted_token_probe.reshape(1, slots_local, group, width)
    decode_state = attend(
        empty_state(1, slots_local, group, width), single, earlier_stored_pairs, None
    )
    live = (jnp.arange(CAP * BLK) < held_blocks * BLK)[None, :]
    decode_state = attend(decode_state, single, cache, live)
    merged = combined_all((decode_state[0], decode_state[1], decode_state[2]), "inst", combine)
    own_scores = jnp.einsum(
        "rkgd,kd->rkg", single, emitted_token_pair[0], preferred_element_type=jnp.float32
    ) * width ** (-0.5)
    highest = jnp.maximum(merged[0], own_scores)
    left = jnp.exp(merged[0] - highest)
    right = jnp.exp(own_scores - highest)
    total = merged[1] * left + right
    own_weight = lax.optimization_barrier(right.astype(jnp.bfloat16)).astype(jnp.float32)
    own_value = emitted_token_pair[1].astype(jnp.float32)
    weighted = merged[2] * left[..., None] + own_weight[..., None] * own_value[None, :, None, :]
    decode_attention = (weighted / total[..., None]).astype(jnp.bfloat16).reshape(heads, width)
    return (span_hidden, cache[None], decode_attention)


def swapped(value, axis, distance):
    size = lax.axis_size(axis)
    return lax.ppermute(value, axis, [(i, i ^ distance) for i in range(size)])


def vmem(count=1):
    return [pl.BlockSpec(memory_space=pltpu.VMEM)] * count


def smem(count=1):
    return [pl.BlockSpec(memory_space=pltpu.SMEM)] * count


def hbm(count=1):
    return [pl.BlockSpec(memory_space=pltpu.HBM)] * count


def anywhere(count=1):
    return [pl.BlockSpec(memory_space=pl.ANY)] * count


def split_pairs_kernel(away, me, fresh, prefix, out):
    rows = fresh.shape[0]
    for y in range(2):

        @pl.when(me[0] >> 2 == y)
        def _():
            s = y ^ away
            for part, start in ((fresh, 0), (prefix, rows)):
                size = part.shape[0]
                out[1, start : start + size] = part[:, 1, s, :]
                for at in range(0, size, BLK):
                    block = part[at : at + BLK, 0, s, :]
                    out[0, start + at : start + at + BLK] = block.T


def split_pairs(away, me, fresh, prefix, after):
    def kernel(me, fresh, prefix, *refs):
        split_pairs_kernel(away, me, fresh, prefix, refs[-1])

    held, width = fresh.shape[0] + prefix.shape[0], fresh.shape[3]
    return pl.pallas_call(
        kernel,
        out_shape=jax.ShapeDtypeStruct((2, held, width), jnp.bfloat16),
        in_specs=smem() + vmem(2) + anywhere(len(after)),
        out_specs=vmem()[0],
        compiler_params=pltpu.CompilerParams(vmem_limit_bytes=24 * 1024 * 1024),
        name="split_pairs",
    )(me, fresh, prefix, *after)


def split_queries_kernel(group, me, queries, own_ref, send_ref):
    chunk_rows = queries.shape[0] // CHUNKS

    def place(out, s):
        for k in range(CHUNKS):
            for g in range(group):
                out[k, g * chunk_rows : (g + 1) * chunk_rows] = queries[
                    k * chunk_rows : (k + 1) * chunk_rows, s * group + g, :
                ]

    for y in range(2):

        @pl.when(me[0] >> 2 == y)
        def _():
            place(own_ref, y)
            place(send_ref, 1 - y)


def split_queries(me, queries, after):
    rows, heads, width = queries.shape
    group = heads // 2
    probes = jax.ShapeDtypeStruct((CHUNKS, group * rows // CHUNKS, width), jnp.bfloat16)

    def kernel(me, queries, *refs):
        split_queries_kernel(group, me, queries, *refs[-2:])

    return pl.pallas_call(
        kernel,
        out_shape=[probes, probes],
        in_specs=smem() + vmem() + anywhere(len(after)),
        out_specs=vmem(2),
        compiler_params=pltpu.CompilerParams(vmem_limit_bytes=24 * 1024 * 1024),
        name="split_queries",
    )(me, queries, *after)


EARLY = (0, 1, 4, 5, 2, 3)
LATE = (6, 7)


def prefix_copies(n, piece, rows, keys, values, sems):
    tile = piece.shape[1] - rows
    at = pl.multiple_of(n * tile, tile)
    return [
        pltpu.make_async_copy(
            piece.at[j, pl.ds(rows, tile)], target.at[pl.ds(at, tile)], sems.at[n, j]
        )
        for j, target in enumerate((keys, values))
    ]


class Tiles:
    def __init__(self, tile, scale, queries, keys, values, weights, shift, sums, weighted):
        self.tile, self.part, self.scale = tile, 2 * BLK, scale
        self.queries, self.keys, self.values = queries, keys, values
        self.weights, self.shift, self.sums, self.weighted = weights, shift, sums, weighted

    def scores(self, t, j, rows):
        at = pl.multiple_of(t * self.tile + j * self.part, self.part)
        block = jnp.concatenate(
            [self.keys[pl.ds(at + l, BLK), :] for l in range(0, self.part, BLK)], axis=1
        )
        return jnp.dot(self.queries[pl.ds(*rows)], block, preferred_element_type=jnp.float32)

    def above(self, t, j, rows, latest):
        width = self.shift.shape[1]
        value, shift = self.scores(t, j, rows), self.shift[pl.ds(*rows)]
        blocks = [value[:, l : l + width] - shift for l in range(0, self.part, width)]
        if latest is None:
            return blocks
        column = lax.broadcasted_iota(jnp.int32, blocks[0].shape, 1)
        return [
            jnp.where(column <= latest - (j * self.part + l * width), block, NEG_FILL)
            for l, block in enumerate(blocks)
        ]

    def weigh(self, t, slot, j, rows, latest):
        width = self.shift.shape[1]
        total = self.sums[pl.ds(*rows)]
        for l, block in enumerate(self.above(t, j, rows, latest)):
            weight = jnp.exp2(block * self.scale)
            total += weight
            at = j * self.part + l * width
            self.weights[slot][pl.ds(*rows), at : at + width] = weight.astype(jnp.bfloat16)
        self.sums[pl.ds(*rows)] = total

    def add(self, t, slot, rows):
        at = pl.multiple_of(t * self.tile, self.tile)
        self.weighted[pl.ds(*rows)] += jnp.dot(
            self.weights[slot][pl.ds(*rows)],
            self.values[pl.ds(at, self.tile), :],
            preferred_element_type=jnp.float32,
        )

    def peak(self, t, rows, latest=None, shifted=True):
        width = self.shift.shape[1]
        peak = None
        for j in range(self.tile // self.part):
            if shifted:
                blocks = self.above(t, j, rows, latest)
            else:
                value = self.scores(t, j, rows)
                blocks = [value[:, l : l + width] for l in range(0, self.part, width)]
            for block in blocks:
                peak = block if peak is None else jnp.maximum(peak, block)
        return jnp.max(peak, axis=1, keepdims=True)

    def first(self, rows):
        top = self.peak(0, rows, shifted=False)
        self.shift[pl.ds(*rows)] = jnp.broadcast_to(top, (rows[1], self.shift.shape[1]))
        for name in (self.sums, self.weighted):
            name[pl.ds(*rows)] = jnp.zeros((rows[1], name.shape[1]), jnp.float32)
        for j in range(self.tile // self.part):
            self.weigh(0, 0, j, rows, None)

    def turn(self, t, slot, rows, latest, before):
        parts = self.tile // self.part
        for j in range(parts):
            self.weigh(t, slot, j, rows, latest)
            for n, side in enumerate(before):
                if n * parts // len(before) == j:
                    self.add(t - 1, 1 - slot, side)

    def careful(self, t, rows, latest):
        up = jnp.maximum(self.peak(t, rows, latest), 0.0)
        factor = jnp.exp2(-up * self.scale)
        self.weighted[pl.ds(*rows)] *= factor
        self.sums[pl.ds(*rows)] *= factor
        self.shift[pl.ds(*rows)] += up
        for j in range(self.tile // self.part):
            self.weigh(t, 0, j, rows, latest)
        self.add(t, 0, rows)


def early_kernel(rows, scale, q_ref, *refs):
    pieces = refs[: len(EARLY)]
    shift, sums, weighted, queries, keys, values, even, odd, sems = refs[len(EARLY) :]
    count, half, _ = q_ref.shape
    tile = pieces[0].shape[1] - rows
    copies = [
        prefix_copies(n, piece, rows, keys, values, sems) for n, piece in enumerate(pieces)
    ]

    @pl.when(pl.program_id(0) == 0)
    def _():
        for pair in copies:
            for copy in pair:
                copy.start()

    for n in range(count):
        queries[n * half : (n + 1) * half] = q_ref[n]

    @pl.when(pl.program_id(0) == 0)
    def _():
        for pair in copies:
            for copy in pair:
                copy.wait()

    tiles = Tiles(tile, scale, queries, keys, values, (even, odd), shift, sums, weighted)
    everything = (0, count * half)
    halves = [(n * half, half) for n in range(count)]
    tiles.first(everything)

    def pair(u, carry):
        tiles.turn(2 * u + 1, 1, everything, None, halves)
        tiles.turn(2 * u + 2, 0, everything, None, halves)
        return carry

    lax.fori_loop(0, 2, pair, 0)
    tiles.turn(5, 1, everything, None, halves)
    for side in halves:
        tiles.add(5, 1, side)


def early_attention(queries, pieces, rows):
    chunks, half, width = queries.shape
    held = pieces[0].shape[1]
    tile = held - rows
    step = 2
    state = jax.ShapeDtypeStruct((chunks * half, width), jnp.float32)
    size = step * half
    keys = len(EARLY) * tile
    return pl.pallas_call(
        functools.partial(early_kernel, rows, width ** (-0.5) * LOG2E),
        grid=(chunks // step,),
        out_shape=[state] * 3,
        in_specs=[pl.BlockSpec((step, half, width), lambda i: (i, 0, 0))] + hbm(len(EARLY)),
        out_specs=[pl.BlockSpec((size, width), lambda i: (i, 0))] * 3,
        scratch_shapes=[
            pltpu.VMEM((size, width), jnp.bfloat16),
            pltpu.VMEM((keys, width), jnp.bfloat16),
            pltpu.VMEM((keys, width), jnp.bfloat16),
            pltpu.VMEM((size, tile), jnp.bfloat16),
            pltpu.VMEM((size, tile), jnp.bfloat16),
            pltpu.SemaphoreType.DMA((len(EARLY), 2)),
        ],
        compiler_params=pltpu.CompilerParams(vmem_limit_bytes=24 * 1024 * 1024),
        cost_estimate=pl.CostEstimate(
            flops=2 * 2 * chunks * half * keys * width * 2,
            bytes_accessed=keys * width * 4 + 3 * chunks * half * width * 4,
            transcendentals=chunks * half * keys,
        ),
        name="early_attention",
    )(queries, *[pieces[p] for p in EARLY])


def attention_kernel(waits, chunk, chunk_rows, rows, group, scale, me, own, beside, *refs):
    states, pieces = refs[:3], refs[3:11]
    out_ref = refs[11 + waits]
    queries, keys, values, even, odd, shift, sums, weighted, sems, late_sems = refs[12 + waits :]
    half = own.shape[1]
    held, width = pieces[0].shape[1:]
    tile = held - rows
    y = me[0] >> 2
    own_rows = (pl.multiple_of(y * half, half), half)
    beside_rows = (pl.multiple_of((1 - y) * half, half), half)
    low, high, everything = (0, half), (half, half), (0, 2 * half)
    order = EARLY + LATE

    def fresh_copies(p):
        at = pl.multiple_of(8 * tile + (me[0] ^ p) * rows, rows)
        return [
            pltpu.make_async_copy(
                pieces[p].at[j, pl.ds(0, rows)], target.at[pl.ds(at, rows)], sems.at[p, 2 + j]
            )
            for j, target in enumerate((keys, values))
        ]

    query_copies = [
        pltpu.make_async_copy(source.at[chunk], queries.at[pl.ds(*place)], late_sems.at[n])
        for n, (source, place) in enumerate(((own, own_rows), (beside, beside_rows)))
    ]
    state_copies = [
        pltpu.make_async_copy(
            source.at[pl.ds(chunk * half, half)], target.at[pl.ds(*own_rows)], late_sems.at[2 + n]
        )
        for n, (source, target) in enumerate(zip(states, (shift, sums, weighted)))
    ]
    copies = [prefix_copies(n, pieces[p], rows, keys, values, sems) for n, p in enumerate(order)]
    for copy in query_copies + copies[0] + state_copies:
        copy.start()
    for pair in copies[1:]:
        for copy in pair:
            copy.start()
    for p in range(8):
        for copy in fresh_copies(p):
            copy.start()

    def wait_for(n):
        for copy in prefix_copies(n, pieces[0], rows, keys, values, sems):
            copy.wait()

    tiles = Tiles(tile, scale, queries, keys, values, (even, odd), shift, sums, weighted)
    for copy in query_copies + copies[0]:
        copy.wait()
    tiles.first(beside_rows)

    def pair(u, carry):
        wait_for(2 * u + 1)
        tiles.turn(2 * u + 1, 1, beside_rows, None, [beside_rows])
        wait_for(2 * u + 2)
        tiles.turn(2 * u + 2, 0, beside_rows, None, [beside_rows])
        return carry

    lax.fori_loop(0, 2, pair, 0)
    wait_for(5)
    tiles.turn(5, 1, beside_rows, None, [beside_rows])
    wait_for(6)
    wait_for(7)
    for copy in state_copies:
        copy.wait()
    tiles.turn(6, 0, everything, None, [beside_rows])
    tiles.turn(7, 1, everything, None, [low, high])
    for p in range(8):
        for copy in fresh_copies(p):
            copy.wait()

    def latest(count):
        row = lax.broadcasted_iota(jnp.int32, (count, width), 0)
        last = (me[0] & 3) * rows + chunk * chunk_rows + row % chunk_rows
        return last if count == half else jnp.where(row < half, last, tile)

    tiles.turn(8, 0, everything, latest(2 * half), [low, high])
    tiles.turn(9, 1, high, latest(half), [low, high])
    tiles.add(9, 1, high)

    @pl.when(jnp.logical_not(jnp.max(sums[...]) < LARGEST))
    def _():
        weighted[...] = jnp.zeros(weighted.shape, jnp.float32)
        sums[...] = jnp.zeros(sums.shape, jnp.float32)

        def prefix_tile(t, carry):
            tiles.careful(t, everything, None)
            return carry

        lax.fori_loop(0, 8, prefix_tile, 0)
        tiles.careful(8, everything, latest(2 * half))
        tiles.careful(9, high, latest(half))

    for h in range(2):
        block = slice(h * half, (h + 1) * half)
        total = jnp.sum(sums[block], axis=1, keepdims=True)
        result = (weighted[block] / total).astype(jnp.bfloat16)
        for g in range(group):
            out_ref[y ^ h, :, g * width : (g + 1) * width] = result[
                g * chunk_rows : (g + 1) * chunk_rows
            ]


def chunk_attention(chunk, me, queries, states, pieces, rows, group, so_far, after):
    _, half, width = queries[0].shape
    chunk_rows = half // group
    held = pieces[0].shape[1]
    tile = held - rows
    aliases = {}
    if so_far is not None:
        aliases = {14 + len(after): 0}
        after = after + [so_far]
    return pl.pallas_call(
        functools.partial(
            attention_kernel,
            len(after),
            chunk,
            chunk_rows,
            rows,
            group,
            width ** (-0.5) * LOG2E,
        ),
        grid=(1,),
        out_shape=jax.ShapeDtypeStruct((2, GROUP * chunk_rows, group * width), jnp.bfloat16),
        in_specs=smem() + hbm(13) + anywhere(len(after)),
        out_specs=pl.BlockSpec((2, chunk_rows, group * width), lambda i: (0, chunk % GROUP, 0)),
        input_output_aliases=aliases,
        scratch_shapes=[
            pltpu.VMEM((2 * half, width), jnp.bfloat16),
            pltpu.VMEM((8 * held, width), jnp.bfloat16),
            pltpu.VMEM((8 * held, width), jnp.bfloat16),
            pltpu.VMEM((2 * half, tile), jnp.bfloat16),
            pltpu.VMEM((2 * half, tile), jnp.bfloat16),
            pltpu.VMEM((2 * half, width), jnp.float32),
            pltpu.VMEM((2 * half, width), jnp.float32),
            pltpu.VMEM((2 * half, width), jnp.float32),
            pltpu.SemaphoreType.DMA((8, 4)),
            pltpu.SemaphoreType.DMA((5,)),
        ],
        compiler_params=pltpu.CompilerParams(vmem_limit_bytes=24 * 1024 * 1024),
        cost_estimate=pl.CostEstimate(
            flops=2 * 2 * 2 * half * 8 * held * width * 2 * 2 // 3,
            bytes_accessed=8 * held * width * 4,
            transcendentals=2 * half * 8 * held * 2 // 3,
        ),
        name="chunk_attention",
    )(me, *queries, *states, *pieces, *after)


def away_kernel(offset, here, across, beside, corner, *refs):
    send_ref = refs[-1]

    @pl.when(offset[0] % 2 == 0)
    def _():
        send_ref[0] = across[...]
        send_ref[1] = corner[...]

    @pl.when(offset[0] % 2 == 1)
    def _():
        send_ref[0] = here[...]
        send_ref[1] = beside[...]


def away(offset, parts, after):
    return pl.pallas_call(
        away_kernel,
        out_shape=jax.ShapeDtypeStruct((2, *parts[0].shape), jnp.bfloat16),
        in_specs=smem() + vmem(4) + anywhere(len(after)),
        out_specs=vmem()[0],
        name="away",
    )(offset, *parts, *after)


def merge_kernel(offset, here, across, beside, corner, came, *refs):
    keep_ref, send_ref = refs[-2:]
    sides = ((here, across), (beside, corner))
    for low in range(2):
        for high in range(2):

            @pl.when(offset[0] == low + 2 * high)
            def _():
                for r, target in ((high, keep_ref), (1 - high, send_ref)):
                    total = sides[r][low][...].astype(jnp.float32) + came[r].astype(jnp.float32)
                    target[...] = total.astype(target.dtype)


def merge(offset, parts, came, after):
    return pl.pallas_call(
        merge_kernel,
        out_shape=[
            jax.ShapeDtypeStruct(parts[0].shape, jnp.float32),
            jax.ShapeDtypeStruct(parts[0].shape, jnp.bfloat16),
        ],
        in_specs=smem() + vmem(5) + anywhere(len(after)),
        out_specs=vmem(2),
        name="merge",
    )(offset, *parts, came, *after)


def finish_kernel(me, keep, came, *refs):
    out_ref = refs[-1]
    columns = keep.shape[2]
    for half in range(2):
        at = pl.multiple_of(((me[0] & 1) ^ half) * columns, columns)
        total = keep[half] + came[half].astype(jnp.float32)
        out_ref[:, pl.ds(at, columns)] = total.astype(out_ref.dtype)


def finish(chunk, me, keep, came, so_far):
    _, rows, columns = keep.shape
    whole = pl.BlockSpec(keep.shape, lambda i: (0, 0, 0))
    operands = [me, keep, came]
    specs = smem() + [whole] * 2
    aliases = {}
    if so_far is not None:
        aliases = {len(operands): 0}
        operands.append(so_far)
        specs += anywhere()
    return pl.pallas_call(
        finish_kernel,
        grid=(1,),
        out_shape=jax.ShapeDtypeStruct((CHUNKS // GROUP * rows, 2 * columns), jnp.bfloat16),
        in_specs=specs,
        out_specs=pl.BlockSpec((rows, 2 * columns), lambda i: (chunk, 0)),
        input_output_aliases=aliases,
        name="finish",
    )(*operands)


def decode_kernel(scale, me, q_ref, last_ref, *refs):
    pieces, out_ref = refs[:8], refs[8]
    q = q_ref[...]
    width = q.shape[1]
    low = me[0] < 4
    last = [jnp.where(low, last_ref[j, 0:1, :], last_ref[j, 1:2, :]) for j in range(2)]
    last = [value.astype(jnp.float32) for value in last]
    running = jnp.sum(q.astype(jnp.float32) * last[0], axis=1, keepdims=True)
    total = jnp.ones_like(running)
    weighted = jnp.broadcast_to(last[1], (q.shape[0], width))
    for piece in pieces:
        scores = jnp.concatenate(
            [
                jnp.dot(q, piece[0, at : at + BLK], preferred_element_type=jnp.float32)
                for at in range(0, piece.shape[1], BLK)
            ],
            axis=1,
        )
        highest = jnp.maximum(running, jnp.max(scores, axis=1, keepdims=True))
        weights = jnp.exp2((scores - highest) * scale)
        factor = jnp.exp2((running - highest) * scale)
        total = total * factor + jnp.sum(weights, axis=1, keepdims=True)
        weighted = weighted * factor + jnp.dot(
            weights.astype(jnp.bfloat16), piece[1], preferred_element_type=jnp.float32
        )
        running = highest
    out_ref[...] = (weighted / total).astype(jnp.bfloat16)


def decode(me, query, last, pieces, after):
    width = query.shape[1]
    held = pieces[0].shape[1]

    def kernel(me, q_ref, last_ref, *refs):
        decode_kernel(width ** (-0.5) * LOG2E, me, q_ref, last_ref, *refs[:8], refs[-1])

    return pl.pallas_call(
        kernel,
        out_shape=jax.ShapeDtypeStruct(query.shape, jnp.bfloat16),
        in_specs=smem() + vmem(10) + anywhere(len(after)),
        out_specs=vmem()[0],
        compiler_params=pltpu.CompilerParams(vmem_limit_bytes=32 * 1024 * 1024),
        cost_estimate=pl.CostEstimate(
            flops=4 * query.shape[0] * width * 8 * held,
            bytes_accessed=8 * held * width * 4,
            transcendentals=query.shape[0] * 8 * held,
        ),
        name="decode",
    )(me, query, last, *pieces, *after)


def pick_kernel(rows, me, member, remaining, *refs):
    pieces, (*outs, held, sems) = refs[:8], refs[-4:]
    count = member.shape[0]
    copies = []
    for p in range(8):
        at = pl.multiple_of((me[0] ^ p) * rows, rows)
        copies.append(
            pltpu.make_async_copy(
                pieces[p].at[:, pl.ds(0, rows)], held.at[:, pl.ds(at, rows)], sems.at[p]
            )
        )
        copies[p].start()
    for out in outs:
        out[...] = jnp.zeros(out.shape, out.dtype)
    for copy in copies:
        copy.wait()
    for b in range(count):
        target = member[b, 0]
        owner = remaining[target]
        spot = jnp.int32(0)
        for before in range(b):
            spot += (member[before, 0] == target).astype(jnp.int32)
        at = pl.multiple_of(spot * BLK, BLK)
        for out, instance in zip(outs, (me[0], me[0] ^ 4)):

            @pl.when(owner == instance)
            def _():
                out[0, pl.ds(at, BLK), :] = held[0, b * BLK : (b + 1) * BLK, :].T
                out[1, pl.ds(at, BLK), :] = held[1, b * BLK : (b + 1) * BLK, :]


def pick_blocks(me, member, remaining, pieces, rows, after):
    width = pieces[0].shape[2]
    shape = jax.ShapeDtypeStruct((2, CAP * BLK, width), jnp.bfloat16)
    return pl.pallas_call(
        functools.partial(pick_kernel, rows),
        out_shape=[shape, shape],
        in_specs=smem(3) + hbm(8) + anywhere(len(after)),
        out_specs=vmem(2),
        scratch_shapes=[
            pltpu.VMEM((2, 8 * rows, width), jnp.bfloat16),
            pltpu.SemaphoreType.DMA((8,)),
        ],
        compiler_params=pltpu.CompilerParams(vmem_limit_bytes=32 * 1024 * 1024),
        name="pick_blocks",
    )(me, member, remaining, *pieces, *after)


def project_kernel(waits, slot, own, beside, across, corner, *refs):
    weights, outs = refs[:4], refs[4 + waits :]
    same = jnp.concatenate([own[0], own[1], across[0], across[1]], axis=0)
    other = jnp.concatenate([beside[1], beside[0], corner[1], corner[0]], axis=0)
    rows = own.shape[1]
    for half in range(2):
        total = jnp.dot(same, weights[2 * half][...], preferred_element_type=jnp.float32)
        total += jnp.dot(other, weights[2 * half + 1][...], preferred_element_type=jnp.float32)
        total = total.astype(jnp.bfloat16)
        for r in range(4):
            outs[r][half] = total[r * rows : (r + 1) * rows]


def project(slot, parts, own_weights, sibling_weights, after):
    _, rows, depth = parts[0].shape
    columns = own_weights.shape[1]
    tile = min(512, columns)
    whole = pl.BlockSpec((2, rows, depth), lambda j, slot: (0, 0, 0))
    same = pl.BlockSpec((depth, tile), lambda j, slot: (slot[0], j))
    other = pl.BlockSpec((depth, tile), lambda j, slot: (1 - slot[0], j))
    out = pl.BlockSpec((2, rows, tile), lambda j, slot: (0, 0, j))
    return pl.pallas_call(
        functools.partial(project_kernel, len(after)),
        grid_spec=pltpu.PrefetchScalarGridSpec(
            num_scalar_prefetch=1,
            grid=(columns // tile,),
            in_specs=[whole] * 4 + [same, other] * 2 + anywhere(len(after)),
            out_specs=[out] * 4,
        ),
        out_shape=[jax.ShapeDtypeStruct((2, rows, columns), jnp.bfloat16)] * 4,
        compiler_params=pltpu.CompilerParams(vmem_limit_bytes=26 * 1024 * 1024),
        cost_estimate=pl.CostEstimate(
            flops=2 * 4 * rows * 2 * depth * 2 * columns,
            bytes_accessed=2 * depth * 2 * columns * 2,
            transcendentals=0,
        ),
        name="project",
    )(slot, *parts, own_weights, own_weights, sibling_weights, sibling_weights, *after)


def on_device_planes(
    fresh_segment_probes,
    fresh_segment_pairs,
    earlier_stored_pairs,
    emitted_token_probe,
    emitted_token_pair,
    final_projection_weights,
    remaining_instance_ids,
    segment_destination_member,
):
    index = lax.axis_index("inst")
    slot = index // 4
    rows, heads, width = fresh_segment_probes.shape
    group = heads // 2
    me = jnp.reshape(index, (1,)).astype(jnp.int32)
    slot_array = jnp.reshape(slot, (1,)).astype(jnp.int32)
    offset = jnp.reshape(lax.axis_index("tp") ^ (index // 2), (1,)).astype(jnp.int32)

    piece = {}
    to_beside = split_pairs(1, me, fresh_segment_pairs, earlier_stored_pairs, [])
    piece[4] = swapped(to_beside, "inst", 4)
    piece[0] = split_pairs(0, me, fresh_segment_pairs, earlier_stored_pairs, [to_beside])
    piece[2] = swapped(piece[0], "inst", 2)
    queries_own, queries_send = split_queries(me, fresh_segment_probes, [piece[0]])
    queries = [queries_own, swapped(queries_send, "inst", 4)]
    piece[6] = swapped(piece[4], "inst", 2)
    for d in (0, 4, 2, 6):
        piece[d + 1] = swapped(piece[d], "inst", 1)
    pieces = [piece[d] for d in range(8)]
    sibling_weights = swapped(final_projection_weights, "inst", 1)

    states = early_attention(queries_own, pieces, rows)

    def attention(k, after):
        own = None
        for chunk in range(k * GROUP, (k + 1) * GROUP):
            own = chunk_attention(
                chunk, me, queries, states, pieces, rows, group, own, after if own is None else []
            )
        return [own] + [swapped(own, "inst", d) for d in (4, 2, 6)]

    def projected(parts, after):
        outs = project(slot_array, parts, final_projection_weights, sibling_weights, after)
        return [outs[0]] + [swapped(outs[i], "inst", d) for i, d in ((1, 4), (2, 2), (3, 6))]

    sums = {}

    def first_step(k, after):
        parts = [partial[k][0], partial[k][2], partial[k][1], partial[k][3]]
        send = away(offset, parts, after)
        sums[k] = (parts, swapped(send, "tp", 1))
        return send

    def second_step(k, after):
        keep, send = merge(offset, *sums[k], after)
        sums[k] = (keep, swapped(send, "tp", 2))
        return send

    gathered, partial = {}, {}
    picked_own, picked_send = pick_blocks(
        me, segment_destination_member, remaining_instance_ids, pieces, rows, []
    )
    picked_beside = swapped(picked_send, "inst", 4)
    token = picked_own
    groups = range(CHUNKS // GROUP)
    for k in groups:
        gathered[k] = attention(k, [token])
        token = gathered[k][0]
    for k in groups:
        partial[k] = projected(gathered[k], [token])
        token = partial[k][0]
        if k == 0:
            decoded = decode(me, emitted_token_probe, emitted_token_pair, pieces, [token])
            token = decoded
    for k in groups:
        token = first_step(k, [token])
    for k in groups:
        token = second_step(k, [token])
    span_hidden = None
    for k in groups:
        span_hidden = finish(k, me, *sums[k], span_hidden)

    first = jnp.where(slot == 0, picked_own, picked_beside)
    second = jnp.where(slot == 0, picked_beside, picked_own)
    cache = jnp.stack([first, second]).transpose(2, 1, 0, 3)

    decoded_beside = swapped(decoded, "inst", 4)
    mine = (jnp.arange(heads) // group == slot)[:, None]
    decode_attention = jnp.where(mine, decoded, decoded_beside)
    return (span_hidden, cache[None], decode_attention)


def solution(mesh):
    instances, groups = mesh.shape["inst"], mesh.shape["tp"]

    def on_device(*arguments):
        slots_local = arguments[1].shape[2]
        tile = arguments[2].shape[0]
        rows = arguments[1].shape[0]
        if instances == 8 and groups == 4 and slots_local == 2 and tile == 4 * rows:
            return on_device_planes(*arguments)
        return on_device_ring(*arguments)

    return jax.shard_map(
        on_device,
        mesh=mesh,
        in_specs=(
            P("inst", "tp", None),
            P("inst", None, "tp", None),
            P("inst", None, "tp", None),
            P("tp", None),
            P(None, "tp", None),
            P("tp", "inst"),
            P(),
            P(),
        ),
        out_specs=(P("inst", "tp"), P("inst", None, None, "tp", None), P("tp", None)),
        check_vma=False,
    )
```

profile of v0, /device:TPU:0, one launch (start us, length us, event | category | flops | bytes accessed | tf_op | source)
XLA Modules:
  0.0 294.5 jit_solution(4009417154721498155)
XLA Ops:
  8.6 3.2 %split_pairs.3.refs_0_.refs_3_ = bf16[2,1280,128]{2,1,0:T(8,128)(2,1)S(1)} custom-call(s32[1]{0:T(128)} %bitcast.me, bf16[256,2,2,128]{3,2,1,0:T(2,128)(2,1)S(1)} %copy-done.4, bf16[1024,2,2,128]{3,2,1,0:T(2,128)(2,1)S(1)} %copy-done.2, bf16[2,1280,128]{2,1,0:T(8,128)(2,1)S(1)} %split_pairs.2.refs_0_), custom_call_target="tpu_custom_call" | custom-call | tf_op jit(solution)/shard_map/split_pairs/pallas_call | solution.py:214
  13.4 9.9 %collective-permute-done.2.refs_2_.refs_4_.refs_7_ = bf16[2,1280,128]{2,1,0:T(8,128)(2,1)S(1)} collective-permute-done((bf16[2,1280,128]{2,1,0:T(8,128)(2,1)S(1)}, bf16[2,1280,128]{2,1,0:T(8,128)(2,1)S(1)}, u32[]{:S(2)}, u32[]{:S(2)}) %collective-permute-start.2) | collective-permute-done | bytes 655392 | tf_op jit(solution)/shard_map/ppermute | solution.py:175
  25.1 4.5 %collective-permute-done.4.refs_4_.refs_2_.refs_5_ = bf16[2,1280,128]{2,1,0:T(8,128)(2,1)S(1)} collective-permute-done((bf16[2,1280,128]{2,1,0:T(8,128)(2,1)S(1)}, bf16[2,1280,128]{2,1,0:T(8,128)(2,1)S(1)}, u32[]{:S(2)}, u32[]{:S(2)}) %collective-permute-start.4) | collective-permute-done | bytes 655392 | tf_op jit(solution)/shard_map/ppermute | solution.py:175
  33.8 8.5 %collective-permute-done.6.refs_6_.refs_9_ = bf16[2,1280,128]{2,1,0:T(8,128)(2,1)} collective-permute-done((bf16[2,1280,128]{2,1,0:T(8,128)(2,1)S(1)}, bf16[2,1280,128]{2,1,0:T(8,128)(2,1)}, u32[]{:S(2)}, u32[]{:S(2)}) %collective-permute-start.6) | collective-permute-done | bytes 655392 | tf_op jit(solution)/shard_map/ppermute | solution.py:175
  42.3 18.6 %early_attention.1 = (f32[2048,128]{1,0:T(8,128)S(1)}, f32[2048,128]{1,0:T(8,128)S(1)}, f32[2048,128]{1,0:T(8,128)S(1)}) custom-call(bf16[4,512,128]{2,1,0:T(8,128)(2,1)S(1)} %get-tuple-element.22.q_ref.own, bf16[2,1280,128]{2,1,0:T(8,128)(2,1)S(1)} %split_pairs.3.refs_0_.refs_3_, bf16[2,1280,128]{2,1,0:T(8,128)(2,1)S(1)} %collective-permute-done.1.refs_1_.refs_4_, ...), custom_call_target="tpu_custom_call" | custom-call | flops 12884901888 | bytes 6291456 | tf_op jit(solution)/shard_map/early_attention/pallas_call | solution.py:406
  60.9 3.1 %pick_blocks.1 = (bf16[2,1024,128]{2,1,0:T(8,128)(2,1)S(1)}, bf16[2,1024,128]{2,1,0:T(8,128)(2,1)S(1)}) custom-call(s32[1]{0:T(128)} %bitcast.me, s32[16,1]{1,0:T(8,128)S(1)} %copy.14.member, s32[4]{0:T(128)S(1)} %copy-done.9, bf16[2,1280,128]{2,1,0:T(8,128)(2,1)S(1)} %split_pairs.3.refs_0_.refs_3_, ...), custom_call_target="tpu_custom_call" | custom-call | tf_op jit(solution)/shard_map/pick_blocks/pallas_call | solution.py:744
  64.0 31.9 %chunk_attention.4.refs_11_ = bf16[2,128,1024]{2,1,0:T(8,128)(2,1)S(1)} custom-call(s32[1]{0:T(128)} %bitcast.me, bf16[4,512,128]{2,1,0:T(8,128)(2,1)S(1)} %copy-done.13, bf16[4,512,128]{2,1,0:T(8,128)(2,1)S(1)} %collective-permute-done.beside, f32[2048,128]{1,0:T(8,128)S(1)} %get-tuple-element.24.refs_0_, f32[2048,128]{1,0:T(8,128)S(1)} %get-tuple-element.25.refs_1_, ...), custom_call_target="tpu_custom_call" | custom-call | flops 7158278656 | bytes 5242880 | tf_op jit(solution)/shard_map/chunk_attention/pallas_call | solution.py:542
  96.0 18.6 %chunk_attention.5.refs_11_.own = bf16[2,128,1024]{2,1,0:T(8,128)(2,1)S(1)} custom-call(s32[1]{0:T(128)} %bitcast.me, bf16[4,512,128]{2,1,0:T(8,128)(2,1)S(1)} %copy-done.13, bf16[4,512,128]{2,1,0:T(8,128)(2,1)S(1)} %collective-permute-done.beside, f32[2048,128]{1,0:T(8,128)S(1)} %get-tuple-element.24.refs_0_, ...), custom_call_target="tpu_custom_call", output_to_operand_aliasing={{}: (14, {})} | custom-call | flops 7158278656 | bytes 5242880 | tf_op jit(solution)/shard_map/chunk_attention/pallas_call | solution.py:542
  114.9 3.2 %collective-permute-start.14 = (bf16[2,128,1024]{2,1,0:T(8,128)(2,1)S(1)}, bf16[2,128,1024]{2,1,0:T(8,128)(2,1)S(1)}, u32[]{:S(2)}, u32[]{:S(2)}) collective-permute-start(bf16[2,128,1024]{2,1,0:T(8,128)(2,1)S(1)} %chunk_attention.5.refs_11_.own), channel_id=1, source_target_pairs={{0,24},{4,28},{8,16},{12,20},{16,8},{20,12},{24,0},{28,4},{1,25},{... | collective-permute-start | bytes 1572872 | tf_op jit(solution)/shard_map/ppermute | solution.py:175
  118.1 18.3 %chunk_attention.6.refs_11_ = bf16[2,128,1024]{2,1,0:T(8,128)(2,1)S(1)} custom-call(s32[1]{0:T(128)} %bitcast.me, bf16[4,512,128]{2,1,0:T(8,128)(2,1)S(1)} %copy-done.13, bf16[4,512,128]{2,1,0:T(8,128)(2,1)S(1)} %collective-permute-done.beside, f32[2048,128]{1,0:T(8,128)S(1)} %get-tuple-element.24.refs_0_, f32[2048,128]{1,0:T(8,128)S(1)} %get-tuple-element.25.refs_1_, ...), custom_call_target="tpu_custom_call" | custom-call | flops 7158278656 | bytes 5242880 | tf_op jit(solution)/shard_map/chunk_attention/pallas_call | solution.py:542
  136.4 12.4 %chunk_attention.7.refs_4_.own = bf16[2,128,1024]{2,1,0:T(8,128)(2,1)S(1)} custom-call(s32[1]{0:T(128)} %bitcast.me, bf16[4,512,128]{2,1,0:T(8,128)(2,1)S(1)} %copy-done.13, bf16[4,512,128]{2,1,0:T(8,128)(2,1)S(1)} %collective-permute-done.beside, f32[2048,128]{1,0:T(8,128)S(1)} %get-tuple-element.24.refs_0_, ...), custom_call_target="tpu_custom_call", output_to_operand_aliasing={{}: (14, {})} | custom-call | flops 7158278656 | bytes 5242880 | tf_op jit(solution)/shard_map/chunk_attention/pallas_call | solution.py:542
  148.8 19.9 %collective-permute-start.10 = (bf16[2,128,1024]{2,1,0:T(8,128)(2,1)S(1)}, bf16[2,128,1024]{2,1,0:T(8,128)(2,1)S(1)}, u32[]{:S(2)}, u32[]{:S(2)}) collective-permute-start(bf16[2,128,1024]{2,1,0:T(8,128)(2,1)S(1)} %chunk_attention.7.refs_4_.own), channel_id=1, source_target_pairs={{0,24},{4,28},{8,16},{12,20},{16,8},{20,12},{24,0},{28,4},{1,25},{... | collective-permute-start | bytes 1572872 | tf_op jit(solution)/shard_map/ppermute | solution.py:175
  169.4 7.8 %project.2 = (bf16[2,128,1024]{2,1,0:T(8,128)(2,1)S(1)}, bf16[2,128,1024]{2,1,0:T(8,128)(2,1)}, bf16[2,128,1024]{2,1,0:T(8,128)(2,1)S(1)}, bf16[2,128,1024]{2,1,0:T(8,128)(2,1)}) custom-call(s32[1]{0:T(128)} %bitcast.2.slot, bf16[2,128,1024]{2,1,0:T(8,128)(2,1)S(1)} %chunk_attention.5.refs_11_.own, bf16[2,128,1024]{2,1,0:T(8,128)(2,1)S(1)} %collective-permute-done.12.beside, ...), custom_call_target="tpu_custom_call" | custom-call | flops 4294967296 | bytes 8388608 | tf_op jit(solution)/shard_map/project/pallas_call | solution.py:779
  180.5 4.2 %decode.1.refs_4_ = bf16[16,128]{1,0:T(8,128)(2,1)S(1)} custom-call(s32[1]{0:T(128)} %bitcast.me, bf16[16,128]{1,0:T(8,128)(2,1)S(1)} %copy-done.7, bf16[2,2,128]{2,1,0:T(2,128)(2,1)S(1)} %copy-done.8, bf16[2,1280,128]{2,1,0:T(8,128)(2,1)S(1)} %split_pairs.3.refs_0_.refs_3_, bf16[2,1280,128]{2,1,0:T(8,128)(2,1)S(1)} %collective-permute-done.1.refs_1_.refs_4_, ...), custom_call_target="tpu_custom_call" | custom-call | flops 83886080 | bytes 5242880 | tf_op jit(solution)/shard_map/decode/pallas_call | solution.py:695
  184.9 3.3 %collective-permute-done.8.beside = bf16[2,128,1024]{2,1,0:T(8,128)(2,1)S(1)} collective-permute-done((bf16[2,128,1024]{2,1,0:T(8,128)(2,1)S(1)}, bf16[2,128,1024]{2,1,0:T(8,128)(2,1)S(1)}, u32[]{:S(2)}, u32[]{:S(2)}) %collective-permute-start.8) | collective-permute-done | bytes 524320 | tf_op jit(solution)/shard_map/ppermute | solution.py:175
  188.2 4.1 %collective-permute-done.9.across = bf16[2,128,1024]{2,1,0:T(8,128)(2,1)S(1)} collective-permute-done((bf16[2,128,1024]{2,1,0:T(8,128)(2,1)S(1)}, bf16[2,128,1024]{2,1,0:T(8,128)(2,1)S(1)}, u32[]{:S(2)}, u32[]{:S(2)}) %collective-permute-start.9) | collective-permute-done | bytes 524320 | tf_op jit(solution)/shard_map/ppermute | solution.py:175
  192.3 7.1 %project.3 = (bf16[2,128,1024]{2,1,0:T(8,128)(2,1)S(1)}, bf16[2,128,1024]{2,1,0:T(8,128)(2,1)S(1)}, bf16[2,128,1024]{2,1,0:T(8,128)(2,1)S(1)}, bf16[2,128,1024]{2,1,0:T(8,128)(2,1)S(1)}) custom-call(s32[1]{0:T(128)} %bitcast.2.slot, bf16[2,128,1024]{2,1,0:T(8,128)(2,1)S(1)} %chunk_attention.7.refs_4_.own, ...), custom_call_target="tpu_custom_call" | custom-call | flops 4294967296 | bytes 8388608 | tf_op jit(solution)/shard_map/project/pallas_call | solution.py:779
  206.1 9.2 %collective-permute-done.20.corner = bf16[2,128,1024]{2,1,0:T(8,128)(2,1)} collective-permute-done((bf16[2,128,1024]{2,1,0:T(8,128)(2,1)}, bf16[2,128,1024]{2,1,0:T(8,128)(2,1)}, u32[]{:S(2)}, u32[]{:S(2)}) %collective-permute-start.20) | collective-permute-done | bytes 524320 | tf_op jit(solution)/shard_map/ppermute | solution.py:175
  217.9 6.1 %collective-permute-done.15.across = bf16[2,128,1024]{2,1,0:T(8,128)(2,1)S(1)} collective-permute-done((bf16[2,128,1024]{2,1,0:T(8,128)(2,1)S(1)}, bf16[2,128,1024]{2,1,0:T(8,128)(2,1)S(1)}, u32[]{:S(2)}, u32[]{:S(2)}) %collective-permute-start.15) | collective-permute-done | bytes 524320 | tf_op jit(solution)/shard_map/ppermute | solution.py:175
  224.8 8.0 %collective-permute-done.17.corner = bf16[2,128,1024]{2,1,0:T(8,128)(2,1)} collective-permute-done((bf16[2,128,1024]{2,1,0:T(8,128)(2,1)S(1)}, bf16[2,128,1024]{2,1,0:T(8,128)(2,1)}, u32[]{:S(2)}, u32[]{:S(2)}) %collective-permute-start.17) | collective-permute-done | bytes 524320 | tf_op jit(solution)/shard_map/ppermute | solution.py:175
  237.5 3.4 %merge.2 = (f32[2,128,1024]{2,1,0:T(8,128)}, bf16[2,128,1024]{2,1,0:T(8,128)(2,1)}) custom-call(s32[1]{0:T(128)} %bitcast.1.offset, bf16[2,128,1024]{2,1,0:T(8,128)(2,1)} %copy-done, bf16[2,128,1024]{2,1,0:T(8,128)(2,1)} %copy-done.15, bf16[2,128,1024]{2,1,0:T(8,128)(2,1)} %collective-permute-done.19.beside, ...), custom_call_target="tpu_custom_call" | custom-call | tf_op jit(solution)/shard_map/merge/pallas_call | solution.py:617
  243.5 23.5 %collective-permute-done.21.came = bf16[2,2,128,1024]{3,2,1,0:T(8,128)(2,1)S(1)} collective-permute-done((bf16[2,2,128,1024]{3,2,1,0:T(8,128)(2,1)}, bf16[2,2,128,1024]{3,2,1,0:T(8,128)(2,1)S(1)}, u32[]{:S(2)}, u32[]{:S(2)}) %collective-permute-start.21) | collective-permute-done | bytes 1048608 | tf_op jit(solution)/shard_map/ppermute | solution.py:175
  268.0 3.2 %merge.3 = (f32[2,128,1024]{2,1,0:T(8,128)}, bf16[2,128,1024]{2,1,0:T(8,128)(2,1)}) custom-call(s32[1]{0:T(128)} %bitcast.1.offset, bf16[2,128,1024]{2,1,0:T(8,128)(2,1)} %copy-done.1, bf16[2,128,1024]{2,1,0:T(8,128)(2,1)} %copy-done.16, bf16[2,128,1024]{2,1,0:T(8,128)(2,1)} %collective-permute-done.16.beside, ...), custom_call_target="tpu_custom_call" | custom-call | tf_op jit(solution)/shard_map/merge/pallas_call | solution.py:617
  280.2 11.9 %collective-permute-done.23.came = bf16[2,128,1024]{2,1,0:T(8,128)(2,1)} collective-permute-done((bf16[2,128,1024]{2,1,0:T(8,128)(2,1)}, bf16[2,128,1024]{2,1,0:T(8,128)(2,1)}, u32[]{:S(2)}, u32[]{:S(2)}) %collective-permute-start.23) | collective-permute-done | bytes 524320 | tf_op jit(solution)/shard_map/ppermute | solution.py:175
  (94 shorter events, 49.5 us)
Async XLA Ops:
  5.6 17.8 %collective-permute-start.2 = (bf16[2,1280,128]{2,1,0:T(8,128)(2,1)S(1)}, bf16[2,1280,128]{2,1,0:T(8,128)(2,1)S(1)}, u32[]{:S(2)}, u32[]{:S(2)}) collective-permute-start(bf16[2,1280,128]{2,1,0:T(8,128)(2,1)S(1)} %split_pairs.2.refs_0_), channel_id=1, source_target_pairs={{0,16},{4,20},{8,24},{12,28},{16,0},{20,4},{24,8},{28,12},{1,17},{... | collective-permute-start | bytes 1966088 | tf_op jit(solution)/shard_map/ppermute | solution.py:175
  11.8 17.7 %collective-permute-start.4 = (bf16[2,1280,128]{2,1,0:T(8,128)(2,1)S(1)}, bf16[2,1280,128]{2,1,0:T(8,128)(2,1)S(1)}, u32[]{:S(2)}, u32[]{:S(2)}) collective-permute-start(bf16[2,1280,128]{2,1,0:T(8,128)(2,1)S(1)} %split_pairs.3.refs_0_.refs_3_), channel_id=1, source_target_pairs={{0,8},{4,12},{8,0},{12,4},{16,24},{20,28},{24,16},{28,20},{1,9},{5... | collective-permute-start | bytes 1966088 | tf_op jit(solution)/shard_map/ppermute | solution.py:175
  13.4 20.4 %collective-permute-start.1 = (bf16[2,1280,128]{2,1,0:T(8,128)(2,1)S(1)}, bf16[2,1280,128]{2,1,0:T(8,128)(2,1)S(1)}, u32[]{:S(2)}, u32[]{:S(2)}) collective-permute-start(bf16[2,1280,128]{2,1,0:T(8,128)(2,1)S(1)} %split_pairs.3.refs_0_.refs_3_), channel_id=1, source_target_pairs={{0,4},{4,0},{8,12},{12,8},{16,20},{20,16},{24,28},{28,24},{1,5},{5... | collective-permute-start | bytes 1966088 | tf_op jit(solution)/shard_map/ppermute | solution.py:175
  23.3 18.9 %collective-permute-start.6 = (bf16[2,1280,128]{2,1,0:T(8,128)(2,1)S(1)}, bf16[2,1280,128]{2,1,0:T(8,128)(2,1)}, u32[]{:S(2)}, u32[]{:S(2)}) collective-permute-start(bf16[2,1280,128]{2,1,0:T(8,128)(2,1)S(1)} %collective-permute-done.2.refs_2_.refs_4_.refs_7_), channel_id=1, source_target_pairs={{0,8},{4,12},{8,0},{12,4},{16,24},{20,28},{24,16},{28,20},{1,9},{5... | collective-permute-start | bytes 1966088 | tf_op jit(solution)/shard_map/ppermute | solution.py:175
  30.1 139.3 %collective-permute-start.11 = (bf16[2048,1024]{1,0:T(8,128)(2,1)}, bf16[2048,1024]{1,0:T(8,128)(2,1)}, u32[]{:S(2)}, u32[]{:S(2)}) collective-permute-start(bf16[2048,1024]{1,0:T(8,128)(2,1)} %refs_1_.3), channel_id=1, source_target_pairs={{0,4},{4,0},{8,12},{12,8},{16,20},{20,16},{24,28},{28,24},{1,5},{5... | collective-permute-start | bytes 12582920 | tf_op jit(solution)/shard_map/ppermute | solution.py:175
  33.8 30.2 %collective-permute-start = (bf16[4,512,128]{2,1,0:T(8,128)(2,1)}, bf16[4,512,128]{2,1,0:T(8,128)(2,1)S(1)}, u32[]{:S(2)}, u32[]{:S(2)}) collective-permute-start(bf16[4,512,128]{2,1,0:T(8,128)(2,1)} %copy-done.14), channel_id=1, source_target_pairs={{0,16},{4,20},{8,24},{12,28},{16,0},{20,4},{24,8},{28,12},{1,17},{... | collective-permute-start | bytes 1572872 | tf_op jit(solution)/shard_map/ppermute | solution.py:175
  42.2 18.6 %collective-permute-start.7 = (bf16[2,1280,128]{2,1,0:T(8,128)(2,1)}, bf16[2,1280,128]{2,1,0:T(8,128)(2,1)S(1)}, u32[]{:S(2)}, u32[]{:S(2)}) collective-permute-start(bf16[2,1280,128]{2,1,0:T(8,128)(2,1)} %collective-permute-done.6.refs_6_.refs_9_), channel_id=1, source_target_pairs={{0,4},{4,0},{8,12},{12,8},{16,20},{20,16},{24,28},{28,24},{1,5},{5... | collective-permute-start | bytes 1966088 | tf_op jit(solution)/shard_map/ppermute | solution.py:175
  114.6 54.1 %collective-permute-start.12 = (bf16[2,128,1024]{2,1,0:T(8,128)(2,1)S(1)}, bf16[2,128,1024]{2,1,0:T(8,128)(2,1)S(1)}, u32[]{:S(2)}, u32[]{:S(2)}) collective-permute-start(bf16[2,128,1024]{2,1,0:T(8,128)(2,1)S(1)} %chunk_attention.5.refs_11_.own), channel_id=1, source_target_pairs={{0,16},{4,20},{8,24},{12,28},{16,0},{20,4},{24,8},{28,12},{1,17},{... | collective-permute-start | bytes 1572872 | tf_op jit(solution)/shard_map/ppermute | solution.py:175
  114.9 53.8 %collective-permute-start.13 = (bf16[2,128,1024]{2,1,0:T(8,128)(2,1)S(1)}, bf16[2,128,1024]{2,1,0:T(8,128)(2,1)S(1)}, u32[]{:S(2)}, u32[]{:S(2)}) collective-permute-start(bf16[2,128,1024]{2,1,0:T(8,128)(2,1)S(1)} %chunk_attention.5.refs_11_.own), channel_id=1, source_target_pairs={{0,8},{4,12},{8,0},{12,4},{16,24},{20,28},{24,16},{28,20},{1,9},{5... | collective-permute-start | bytes 1572872 | tf_op jit(solution)/shard_map/ppermute | solution.py:175
  114.9 54.4 %collective-permute-start.14 = (bf16[2,128,1024]{2,1,0:T(8,128)(2,1)S(1)}, bf16[2,128,1024]{2,1,0:T(8,128)(2,1)S(1)}, u32[]{:S(2)}, u32[]{:S(2)}) collective-permute-start(bf16[2,128,1024]{2,1,0:T(8,128)(2,1)S(1)} %chunk_attention.5.refs_11_.own), channel_id=1, source_target_pairs={{0,24},{4,28},{8,16},{12,20},{16,8},{20,12},{24,0},{28,4},{1,25},{... | collective-permute-start | bytes 1572872 | tf_op jit(solution)/shard_map/ppermute | solution.py:175
  148.8 36.0 %collective-permute-start.10 = (bf16[2,128,1024]{2,1,0:T(8,128)(2,1)S(1)}, bf16[2,128,1024]{2,1,0:T(8,128)(2,1)S(1)}, u32[]{:S(2)}, u32[]{:S(2)}) collective-permute-start(bf16[2,128,1024]{2,1,0:T(8,128)(2,1)S(1)} %chunk_attention.7.refs_4_.own), channel_id=1, source_target_pairs={{0,24},{4,28},{8,16},{12,20},{16,8},{20,12},{24,0},{28,4},{1,25},{... | collective-permute-start | bytes 1572872 | tf_op jit(solution)/shard_map/ppermute | solution.py:175
  168.7 19.5 %collective-permute-start.8 = (bf16[2,128,1024]{2,1,0:T(8,128)(2,1)S(1)}, bf16[2,128,1024]{2,1,0:T(8,128)(2,1)S(1)}, u32[]{:S(2)}, u32[]{:S(2)}) collective-permute-start(bf16[2,128,1024]{2,1,0:T(8,128)(2,1)S(1)} %chunk_attention.7.refs_4_.own), channel_id=1, source_target_pairs={{0,16},{4,20},{8,24},{12,28},{16,0},{20,4},{24,8},{28,12},{1,17},{... | collective-permute-start | bytes 1572872 | tf_op jit(solution)/shard_map/ppermute | solution.py:175
  168.7 23.6 %collective-permute-start.9 = (bf16[2,128,1024]{2,1,0:T(8,128)(2,1)S(1)}, bf16[2,128,1024]{2,1,0:T(8,128)(2,1)S(1)}, u32[]{:S(2)}, u32[]{:S(2)}) collective-permute-start(bf16[2,128,1024]{2,1,0:T(8,128)(2,1)S(1)} %chunk_attention.7.refs_4_.own), channel_id=1, source_target_pairs={{0,8},{4,12},{8,0},{12,4},{16,24},{20,28},{24,16},{28,20},{1,9},{5... | collective-permute-start | bytes 1572872 | tf_op jit(solution)/shard_map/ppermute | solution.py:175
  177.1 26.4 %collective-permute-start.18 = (bf16[2,128,1024]{2,1,0:T(8,128)(2,1)S(1)}, bf16[2,128,1024]{2,1,0:T(8,128)(2,1)S(1)}, u32[]{:S(2)}, u32[]{:S(2)}) collective-permute-start(bf16[2,128,1024]{2,1,0:T(8,128)(2,1)S(1)} %get-tuple-element.33), channel_id=1, source_target_pairs={{0,8},{4,12},{8,0},{12,4},{16,24},{20,28},{24,16},{28,20},{1,9},{5... | collective-permute-start | bytes 1572872 | tf_op jit(solution)/shard_map/ppermute | solution.py:175
  178.6 27.6 %collective-permute-start.19 = (bf16[2,128,1024]{2,1,0:T(8,128)(2,1)}, bf16[2,128,1024]{2,1,0:T(8,128)(2,1)}, u32[]{:S(2)}, u32[]{:S(2)}) collective-permute-start(bf16[2,128,1024]{2,1,0:T(8,128)(2,1)} %get-tuple-element.34), channel_id=1, source_target_pairs={{0,16},{4,20},{8,24},{12,28},{16,0},{20,4},{24,8},{28,12},{1,17},{... | collective-permute-start | bytes 1572872 | tf_op jit(solution)/shard_map/ppermute | solution.py:175
  184.7 30.6 %collective-permute-start.20 = (bf16[2,128,1024]{2,1,0:T(8,128)(2,1)}, bf16[2,128,1024]{2,1,0:T(8,128)(2,1)}, u32[]{:S(2)}, u32[]{:S(2)}) collective-permute-start(bf16[2,128,1024]{2,1,0:T(8,128)(2,1)} %get-tuple-element.35), channel_id=1, source_target_pairs={{0,24},{4,28},{8,16},{12,20},{16,8},{20,12},{24,0},{28,4},{1,25},{... | collective-permute-start | bytes 1572872 | tf_op jit(solution)/shard_map/ppermute | solution.py:175
  200.2 23.8 %collective-permute-start.15 = (bf16[2,128,1024]{2,1,0:T(8,128)(2,1)S(1)}, bf16[2,128,1024]{2,1,0:T(8,128)(2,1)S(1)}, u32[]{:S(2)}, u32[]{:S(2)}) collective-permute-start(bf16[2,128,1024]{2,1,0:T(8,128)(2,1)S(1)} %get-tuple-element.30), channel_id=1, source_target_pairs={{0,8},{4,12},{8,0},{12,4},{16,24},{20,28},{24,16},{28,20},{1,9},{5... | collective-permute-start | bytes 1572872 | tf_op jit(solution)/shard_map/ppermute | solution.py:175
  202.7 22.1 %collective-permute-start.16 = (bf16[2,128,1024]{2,1,0:T(8,128)(2,1)S(1)}, bf16[2,128,1024]{2,1,0:T(8,128)(2,1)}, u32[]{:S(2)}, u32[]{:S(2)}) collective-permute-start(bf16[2,128,1024]{2,1,0:T(8,128)(2,1)S(1)} %get-tuple-element.31), channel_id=1, source_target_pairs={{0,16},{4,20},{8,24},{12,28},{16,0},{20,4},{24,8},{28,12},{1,17},{... | collective-permute-start | bytes 1572872 | tf_op jit(solution)/shard_map/ppermute | solution.py:175
  203.5 29.3 %collective-permute-start.17 = (bf16[2,128,1024]{2,1,0:T(8,128)(2,1)S(1)}, bf16[2,128,1024]{2,1,0:T(8,128)(2,1)}, u32[]{:S(2)}, u32[]{:S(2)}) collective-permute-start(bf16[2,128,1024]{2,1,0:T(8,128)(2,1)S(1)} %get-tuple-element.32), channel_id=1, source_target_pairs={{0,24},{4,28},{8,16},{12,20},{16,8},{20,12},{24,0},{28,4},{1,25},{... | collective-permute-start | bytes 1572872 | tf_op jit(solution)/shard_map/ppermute | solution.py:175
  217.9 19.5 %collective-permute-start.22 = (bf16[2,2,128,1024]{3,2,1,0:T(8,128)(2,1)}, bf16[2,2,128,1024]{3,2,1,0:T(8,128)(2,1)}, u32[]{:S(2)}, u32[]{:S(2)}) collective-permute-start(bf16[2,2,128,1024]{3,2,1,0:T(8,128)(2,1)} %away.2.refs_0_), channel_id=1, source_target_pairs={{0,1},{1,0},{2,3},{3,2},{4,5},{5,4},{6,7},{7,6},{8,9},{9,8},{10,11... | collective-permute-start | bytes 3145736 | tf_op jit(solution)/shard_map/ppermute | solution.py:175
  235.4 31.6 %collective-permute-start.21 = (bf16[2,2,128,1024]{3,2,1,0:T(8,128)(2,1)}, bf16[2,2,128,1024]{3,2,1,0:T(8,128)(2,1)S(1)}, u32[]{:S(2)}, u32[]{:S(2)}) collective-permute-start(bf16[2,2,128,1024]{3,2,1,0:T(8,128)(2,1)} %away.3.refs_0_), channel_id=1, source_target_pairs={{0,1},{1,0},{2,3},{3,2},{4,5},{5,4},{6,7},{7,6},{8,9},{9,8},{10,11... | collective-permute-start | bytes 3145736 | tf_op jit(solution)/shard_map/ppermute | solution.py:175
  235.4 35.8 %collective-permute-start.25 = (bf16[2,1024,128]{2,1,0:T(8,128)(2,1)S(1)}, bf16[2,1024,128]{2,1,0:T(8,128)(2,1)S(1)}, u32[]{:S(2)}, u32[]{:S(2)}) collective-permute-start(bf16[2,1024,128]{2,1,0:T(8,128)(2,1)S(1)} %copy-done.11), channel_id=1, source_target_pairs={{0,16},{4,20},{8,24},{12,28},{16,0},{20,4},{24,8},{28,12},{1,17},{... | collective-permute-start | bytes 1572872 | tf_op jit(solution)/shard_map/ppermute | solution.py:175
  240.9 36.2 %collective-permute-start.24 = (bf16[2,128,1024]{2,1,0:T(8,128)(2,1)}, bf16[2,128,1024]{2,1,0:T(8,128)(2,1)S(1)}, u32[]{:S(2)}, u32[]{:S(2)}) collective-permute-start(bf16[2,128,1024]{2,1,0:T(8,128)(2,1)} %get-tuple-element.36.refs_0_), channel_id=1, source_target_pairs={{0,2},{1,3},{2,0},{3,1},{4,6},{5,7},{6,4},{7,5},{8,10},{9,11},{10,... | collective-permute-start | bytes 1572872 | tf_op jit(solution)/shard_map/ppermute | solution.py:175
  271.3 20.8 %collective-permute-start.23 = (bf16[2,128,1024]{2,1,0:T(8,128)(2,1)}, bf16[2,128,1024]{2,1,0:T(8,128)(2,1)}, u32[]{:S(2)}, u32[]{:S(2)}) collective-permute-start(bf16[2,128,1024]{2,1,0:T(8,128)(2,1)} %get-tuple-element.38), channel_id=1, source_target_pairs={{0,2},{1,3},{2,0},{3,1},{4,6},{5,7},{6,4},{7,5},{8,10},{9,11},{10,... | collective-permute-start | bytes 1572872 | tf_op jit(solution)/shard_map/ppermute | solution.py:175
  (23 other events, 315.9 us)
where the time goes:
time: 297 us; the launch traced here: 295 us
  Pallas kernels  146 us (49%)
  waiting for transfers between devices  92.8 us (31%)
  starting transfers between devices  45.2 us (15%)
  local copies, waits for them, and re-layouts  8.93 us (3%)
    ppermute x27, waiting for transfers between devices, swapped(): return lax.ppermute(value, axis, [(i, i ^ distance) for i in range(size)])  92.8 us
    pallas_call x4, Pallas kernels, chunk_attention(): pl.pallas_call(functools.partial(attention_kernel, len(after), chunk, chu...  81.2 us
    ppermute x27, starting transfers between devices, swapped(): return lax.ppermute(value, axis, [(i, i ^ distance) for i in range(size)])  45.2 us
    pallas_call x1, Pallas kernels, early_attention(): pl.pallas_call(functools.partial(early_kernel, rows, width ** (-0.5) * LO...  18.6 us
    pallas_call x2, Pallas kernels, project(): pl.pallas_call(functools.partial(project_kernel, len(after)), grid_spec=p...  14.8 us
    unnamed x42, local copies, waits for them, and re-layouts  8.93 us
    pallas_call x2, Pallas kernels, merge(): pl.pallas_call(merge_kernel, out_shape=[jax.ShapeDtypeStruct(parts[0].sha...  6.68 us
    pallas_call x2, Pallas kernels, split_pairs(): pl.pallas_call(kernel, out_shape=jax.ShapeDtypeStruct((2, held, width), j...  5.97 us
  transfers between devices with their start and end apart: 27, of which 13 were waited for; matrix products, arithmetic and copies ran while one was open for 1% of the time, Pallas kernels for 48%

commit v1 on v0

--- a/solution.py
+++ b/solution.py
@@ -14,6 +14,7 @@
 LARGEST = 2.0**100
 CHUNKS = 4
 GROUP = 2
+BRIEF = pl.CostEstimate(flops=1024, bytes_accessed=1024, transcendentals=0)
 
 
 def from_behind(block, axis, distance):
@@ -217,6 +218,7 @@
         in_specs=smem() + vmem(2) + anywhere(len(after)),
         out_specs=vmem()[0],
         compiler_params=pltpu.CompilerParams(vmem_limit_bytes=24 * 1024 * 1024),
+        cost_estimate=BRIEF,
         name="split_pairs",
     )(me, fresh, prefix, *after)
 
@@ -253,6 +255,7 @@
         in_specs=smem() + vmem() + anywhere(len(after)),
         out_specs=vmem(2),
         compiler_params=pltpu.CompilerParams(vmem_limit_bytes=24 * 1024 * 1024),
+        cost_estimate=BRIEF,
         name="split_queries",
     )(me, queries, *after)
 
@@ -418,11 +421,7 @@
             pltpu.SemaphoreType.DMA((len(EARLY), 2)),
         ],
         compiler_params=pltpu.CompilerParams(vmem_limit_bytes=24 * 1024 * 1024),
-        cost_estimate=pl.CostEstimate(
-            flops=2 * 2 * chunks * half * keys * width * 2,
-            bytes_accessed=keys * width * 4 + 3 * chunks * half * width * 4,
-            transcendentals=chunks * half * keys,
-        ),
+        cost_estimate=BRIEF,
         name="early_attention",
     )(queries, *[pieces[p] for p in EARLY])
 
@@ -567,11 +566,7 @@
             pltpu.SemaphoreType.DMA((5,)),
         ],
         compiler_params=pltpu.CompilerParams(vmem_limit_bytes=24 * 1024 * 1024),
-        cost_estimate=pl.CostEstimate(
-            flops=2 * 2 * 2 * half * 8 * held * width * 2 * 2 // 3,
-            bytes_accessed=8 * held * width * 4,
-            transcendentals=2 * half * 8 * held * 2 // 3,
-        ),
+        cost_estimate=BRIEF,
         name="chunk_attention",
     )(me, *queries, *states, *pieces, *after)
 
@@ -596,6 +591,7 @@
         out_shape=jax.ShapeDtypeStruct((2, *parts[0].shape), jnp.bfloat16),
         in_specs=smem() + vmem(4) + anywhere(len(after)),
         out_specs=vmem()[0],
+        cost_estimate=BRIEF,
         name="away",
     )(offset, *parts, *after)
 
@@ -622,6 +618,7 @@
         ],
         in_specs=smem() + vmem(5) + anywhere(len(after)),
         out_specs=vmem(2),
+        cost_estimate=BRIEF,
         name="merge",
     )(offset, *parts, came, *after)
 
@@ -652,6 +649,7 @@
         in_specs=specs,
         out_specs=pl.BlockSpec((rows, 2 * columns), lambda i: (chunk, 0)),
         input_output_aliases=aliases,
+        cost_estimate=BRIEF,
         name="finish",
     )(*operands)
 
@@ -698,11 +696,7 @@
         in_specs=smem() + vmem(10) + anywhere(len(after)),
         out_specs=vmem()[0],
         compiler_params=pltpu.CompilerParams(vmem_limit_bytes=32 * 1024 * 1024),
-        cost_estimate=pl.CostEstimate(
-            flops=4 * query.shape[0] * width * 8 * held,
-            bytes_accessed=8 * held * width * 4,
-            transcendentals=query.shape[0] * 8 * held,
-        ),
+        cost_estimate=BRIEF,
         name="decode",
     )(me, query, last, *pieces, *after)
 
@@ -751,6 +745,7 @@
             pltpu.SemaphoreType.DMA((8,)),
         ],
         compiler_params=pltpu.CompilerParams(vmem_limit_bytes=32 * 1024 * 1024),
+        cost_estimate=BRIEF,
         name="pick_blocks",
     )(me, member, remaining, *pieces, *after)
 
@@ -786,11 +781,7 @@
         ),
         out_shape=[jax.ShapeDtypeStruct((2, rows, columns), jnp.bfloat16)] * 4,
         compiler_params=pltpu.CompilerParams(vmem_limit_bytes=26 * 1024 * 1024),
-        cost_estimate=pl.CostEstimate(
-            flops=2 * 4 * rows * 2 * depth * 2 * columns,
-            bytes_accessed=2 * depth * 2 * columns * 2,
-            transcendentals=0,
-        ),
+        cost_estimate=BRIEF,
         name="project",
     )(slot, *parts, own_weights, own_weights, sibling_weights, sibling_weights, *after)
 
@@ -828,12 +819,15 @@
 
     states = early_attention(queries_own, pieces, rows)
 
-    def attention(k, after):
+    def attention(k, after, between):
         own = None
         for chunk in range(k * GROUP, (k + 1) * GROUP):
+            if between and chunk == (k + 1) * GROUP - 1:
+                after = between(own)
             own = chunk_attention(
-                chunk, me, queries, states, pieces, rows, group, own, after if own is None else []
+                chunk, me, queries, states, pieces, rows, group, own, after
             )
+            after = []
         return [own] + [swapped(own, "inst", d) for d in (4, 2, 6)]
 
     def projected(parts, after):
@@ -854,25 +848,28 @@
         return send
 
     gathered, partial = {}, {}
+    groups = range(CHUNKS // GROUP)
+    gathered[0] = attention(0, [], [])
+    for k in groups[1:]:
+        def between(own, k=k):
+            partial[k - 1] = projected(gathered[k - 1], [own])
+            return [partial[k - 1][0]]
+
+        gathered[k] = attention(k, [gathered[k - 1][0]], between)
+        if k >= 2:
+            first_step(k - 2, [gathered[k][0]])
+            second_step(k - 2, [partial[k - 1][0]])
+    last = len(groups) - 1
+    token = first_step(last - 1, [gathered[last][0]])
+    partial[last] = projected(gathered[last], [token])
+    token = second_step(last - 1, [partial[last][0]])
+    token = first_step(last, [token])
     picked_own, picked_send = pick_blocks(
-        me, segment_destination_member, remaining_instance_ids, pieces, rows, []
+        me, segment_destination_member, remaining_instance_ids, pieces, rows, [token]
     )
     picked_beside = swapped(picked_send, "inst", 4)
-    token = picked_own
-    groups = range(CHUNKS // GROUP)
-    for k in groups:
-        gathered[k] = attention(k, [token])
-        token = gathered[k][0]
-    for k in groups:
-        partial[k] = projected(gathered[k], [token])
-        token = partial[k][0]
-        if k == 0:
-            decoded = decode(me, emitted_token_probe, emitted_token_pair, pieces, [token])
-            token = decoded
-    for k in groups:
-        token = first_step(k, [token])
-    for k in groups:
-        token = second_step(k, [token])
+    decoded = decode(me, emitted_token_probe, emitted_token_pair, pieces, [picked_own])
+    second_step(last, [decoded])
     span_hidden = None
     for k in groups:
         span_hidden = finish(k, me, *sums[k], span_hidden)

time: 297 us -> 302 us (1.017)
  the two profiles are of different devices: /device:TPU:0 before, /device:TPU:3 now
where the time goes in v1:
time: 302 us; the launch traced here: 297 us
  Pallas kernels  127 us (42%)
  starting transfers between devices  83.6 us (28%)
  waiting for transfers between devices  48.7 us (16%)
  local copies, waits for them, and re-layouts  33.8 us (11%)
    ppermute x27, starting transfers between devices, swapped(): return lax.ppermute(value, axis, [(i, i ^ distance) for i in range(size)])  83.6 us
    pallas_call x4, Pallas kernels, chunk_attention(): pl.pallas_call(functools.partial(attention_kernel, len(after), chunk, chu...  63.4 us
    ppermute x27, waiting for transfers between devices, swapped(): return lax.ppermute(value, axis, [(i, i ^ distance) for i in range(size)])  48.7 us
    unnamed x92, local copies, waits for them, and re-layouts  33.8 us
    pallas_call x1, Pallas kernels, early_attention(): pl.pallas_call(functools.partial(early_kernel, rows, width ** (-0.5) * LO...  17.5 us
    pallas_call x2, Pallas kernels, project(): pl.pallas_call(functools.partial(project_kernel, len(after)), grid_spec=p...  15.9 us
    pallas_call x2, Pallas kernels, merge(): pl.pallas_call(merge_kernel, out_shape=[jax.ShapeDtypeStruct(parts[0].sha...  6.48 us
  transfers between devices with their start and end apart: 27, of which 7 were waited for; matrix products, arithmetic and copies ran while one was open for 2% of the time, Pallas kernels for 38%

profile of v1, /device:TPU:3, one launch (start us, length us, event | category | flops | bytes accessed | tf_op | source)
XLA Modules:
  0.0 296.7 jit_solution(674091417669403566)
XLA Ops:
  3.5 2.8 split_pairs.2.refs_0_
  7.6 3.0 %split_pairs.3.refs_0_.refs_3_ = bf16[2,1280,128]{2,1,0:T(8,128)(2,1)S(1)} custom-call(s32[1]{0:T(128)} %bitcast.me, bf16[256,2,2,128]{3,2,1,0:T(2,128)(2,1)S(1)} %copy-done.38, bf16[1024,2,2,128]{3,2,1,0:T(2,128)(2,1)S(1)} %copy-done.32, bf16[2,1280,128]{2,1,0:T(8,128)(2,1)S(1)} %split_pairs.2.refs_0_), custom_call_target="tpu_custom_call" | custom-call | flops 1024 | bytes 1024 | tf_op jit(solution)/shard_map/split_pairs/pallas_call | solution.py:215
  10.9 11.8 %collective-permute-done.2.refs_2_.refs_7_.refs_4_ = bf16[2,1280,128]{2,1,0:T(8,128)(2,1)S(1)} collective-permute-done((bf16[2,1280,128]{2,1,0:T(8,128)(2,1)S(1)}, bf16[2,1280,128]{2,1,0:T(8,128)(2,1)S(1)}, u32[]{:S(2)}, u32[]{:S(2)}) %collective-permute-start.2) | collective-permute-done | bytes 655392 | tf_op jit(solution)/shard_map/ppermute | solution.py:176
  23.8 2.8 collective-permute-done.4.refs_4_.refs_5_.refs_2_
  28.5 12.2 %collective-permute-done.6.refs_9_.refs_6_ = bf16[2,1280,128]{2,1,0:T(8,128)(2,1)S(1)} collective-permute-done((bf16[2,1280,128]{2,1,0:T(8,128)(2,1)S(1)}, bf16[2,1280,128]{2,1,0:T(8,128)(2,1)S(1)}, u32[]{:S(2)}, u32[]{:S(2)}) %collective-permute-start.6) | collective-permute-done | bytes 655392 | tf_op jit(solution)/shard_map/ppermute | solution.py:176
  43.7 17.5 %early_attention.1 = (f32[2048,128]{1,0:T(8,128)S(1)}, f32[2048,128]{1,0:T(8,128)S(1)}, f32[2048,128]{1,0:T(8,128)S(1)}) custom-call(bf16[4,512,128]{2,1,0:T(8,128)(2,1)S(1)} %get-tuple-element.22.q_ref.own, bf16[2,1280,128]{2,1,0:T(8,128)(2,1)S(1)} %split_pairs.3.refs_0_.refs_3_, bf16[2,1280,128]{2,1,0:T(8,128)(2,1)S(1)} %collective-permute-done.1.refs_1_.refs_4_, ...), custom_call_target="tpu_custom_call" | custom-call | flops 1024 | bytes 1024 | tf_op jit(solution)/shard_map/early_attention/pallas_call | solution.py:409
  61.3 13.6 %chunk_attention.4.refs_11_ = bf16[2,128,1024]{2,1,0:T(8,128)(2,1)} custom-call(s32[1]{0:T(128)} %bitcast.me, bf16[4,512,128]{2,1,0:T(8,128)(2,1)S(1)} %get-tuple-element.22.q_ref.own, bf16[4,512,128]{2,1,0:T(8,128)(2,1)S(1)} %collective-permute-done.beside, f32[2048,128]{1,0:T(8,128)S(1)} %get-tuple-element.24.refs_0_, ...), custom_call_target="tpu_custom_call" | custom-call | flops 1024 | bytes 1024 | tf_op jit(solution)/shard_map/chunk_attention/pallas_call | solution.py:541
  75.1 15.4 %chunk_attention.5.refs_11_.own = bf16[2,128,1024]{2,1,0:T(8,128)(2,1)} custom-call(s32[1]{0:T(128)} %bitcast.me, bf16[4,512,128]{2,1,0:T(8,128)(2,1)S(1)} %get-tuple-element.22.q_ref.own, bf16[4,512,128]{2,1,0:T(8,128)(2,1)S(1)} %collective-permute-done.beside, f32[2048,128]{1,0:T(8,128)S(1)} %get-tuple-element.24.refs_0_, ...), custom_call_target="tpu_custom_call", output_to_operand_aliasing={{}: (14, {})} | custom-call | flops 1024 | bytes 1024 | tf_op jit(solution)/shard_map/chunk_attention/pallas_call | solution.py:541
  102.2 21.0 %chunk_attention.6.refs_4_.refs_12_ = bf16[2,128,1024]{2,1,0:T(8,128)(2,1)} custom-call(s32[1]{0:T(128)} %bitcast.me, bf16[4,512,128]{2,1,0:T(8,128)(2,1)S(1)} %copy-done.24, bf16[4,512,128]{2,1,0:T(8,128)(2,1)S(1)} %copy-done.27, f32[2048,128]{1,0:T(8,128)S(1)} %copy-done.15, f32[2048,128]{1,0:T(8,128)S(1)} %copy-done.18, f32[2048,128]{1,0:T(8,128)S(1)} %copy-done.21, ...), custom_call_target="tpu_custom_call" | custom-call | flops 1024 | bytes 1024 | tf_op jit(solution)/shard_map/chunk_attention/pallas_call | solution.py:541
  123.3 8.0 %project.2 = (bf16[2,128,1024]{2,1,0:T(8,128)(2,1)S(1)}, bf16[2,128,1024]{2,1,0:T(8,128)(2,1)}, bf16[2,128,1024]{2,1,0:T(8,128)(2,1)}, bf16[2,128,1024]{2,1,0:T(8,128)(2,1)}) custom-call(s32[1]{0:T(128)} %bitcast.2.slot, bf16[2,128,1024]{2,1,0:T(8,128)(2,1)} %chunk_attention.5.refs_11_.own, bf16[2,128,1024]{2,1,0:T(8,128)(2,1)} %collective-permute-done.8.beside, ...), custom_call_target="tpu_custom_call" | custom-call | flops 1024 | bytes 1024 | tf_op jit(solution)/shard_map/project/pallas_call | solution.py:774
  144.8 13.4 %chunk_attention.7.refs_0_.own = bf16[2,128,1024]{2,1,0:T(8,128)(2,1)} custom-call(s32[1]{0:T(128)} %bitcast.me, bf16[4,512,128]{2,1,0:T(8,128)(2,1)S(1)} %copy-done.25, bf16[4,512,128]{2,1,0:T(8,128)(2,1)S(1)} %copy-done.28, f32[2048,128]{1,0:T(8,128)S(1)} %copy-done.16, f32[2048,128]{1,0:T(8,128)S(1)} %copy-done.19, ...), custom_call_target="tpu_custom_call", output_to_operand_aliasing={{}: (15, {})} | custom-call | flops 1024 | bytes 1024 | tf_op jit(solution)/shard_map/chunk_attention/pallas_call | solution.py:541
  163.5 38.0 %collective-permute-start.21 = (bf16[2,2,128,1024]{3,2,1,0:T(8,128)(2,1)}, bf16[2,2,128,1024]{3,2,1,0:T(8,128)(2,1)}, u32[]{:S(2)}, u32[]{:S(2)}) collective-permute-start(bf16[2,2,128,1024]{3,2,1,0:T(8,128)(2,1)} %away.2.refs_4_), channel_id=1, source_target_pairs={{0,1},{1,0},{2,3},{3,2},{4,5},{5,4},{6,7},{7,6},{8,9},{9,8},{10,11... | collective-permute-start | bytes 3145736 | tf_op jit(solution)/shard_map/ppermute | solution.py:176
  204.9 7.9 %project.3 = (bf16[2,128,1024]{2,1,0:T(8,128)(2,1)S(1)}, bf16[2,128,1024]{2,1,0:T(8,128)(2,1)}, bf16[2,128,1024]{2,1,0:T(8,128)(2,1)}, bf16[2,128,1024]{2,1,0:T(8,128)(2,1)}) custom-call(s32[1]{0:T(128)} %bitcast.2.slot, bf16[2,128,1024]{2,1,0:T(8,128)(2,1)} %chunk_attention.7.refs_0_.own, bf16[2,128,1024]{2,1,0:T(8,128)(2,1)} %collective-permute-done.12.beside, ...), custom_call_target="tpu_custom_call" | custom-call | flops 1024 | bytes 1024 | tf_op jit(solution)/shard_map/project/pallas_call | solution.py:774
  216.3 3.2 %merge.2 = (f32[2,128,1024]{2,1,0:T(8,128)}, bf16[2,128,1024]{2,1,0:T(8,128)(2,1)}) custom-call(s32[1]{0:T(128)} %bitcast.1.offset, bf16[2,128,1024]{2,1,0:T(8,128)(2,1)} %copy-done.29, bf16[2,128,1024]{2,1,0:T(8,128)(2,1)} %collective-permute-done.15.across, bf16[2,128,1024]{2,1,0:T(8,128)(2,1)} %collective-permute-done.16.beside, ...), custom_call_target="tpu_custom_call" | custom-call | flops 1024 | bytes 1024 | tf_op jit(solution)/shard_map/merge/pallas_call | solution.py:613
  222.0 7.3 %collective-permute-done.19.beside = bf16[2,128,1024]{2,1,0:T(8,128)(2,1)} collective-permute-done((bf16[2,128,1024]{2,1,0:T(8,128)(2,1)}, bf16[2,128,1024]{2,1,0:T(8,128)(2,1)}, u32[]{:S(2)}, u32[]{:S(2)}) %collective-permute-start.19) | collective-permute-done | bytes 524320 | tf_op jit(solution)/shard_map/ppermute | solution.py:176
  229.3 2.6 away.3.refs_8_
  231.9 17.8 %collective-permute-start.22 = (bf16[2,2,128,1024]{3,2,1,0:T(8,128)(2,1)}, bf16[2,2,128,1024]{3,2,1,0:T(8,128)(2,1)}, u32[]{:S(2)}, u32[]{:S(2)}) collective-permute-start(bf16[2,2,128,1024]{3,2,1,0:T(8,128)(2,1)} %away.3.refs_8_), channel_id=1, source_target_pairs={{0,1},{1,0},{2,3},{3,2},{4,5},{5,4},{6,7},{7,6},{8,9},{9,8},{10,11... | collective-permute-start | bytes 3145736 | tf_op jit(solution)/shard_map/ppermute | solution.py:176
  249.8 4.5 %collective-permute-start.24 = (bf16[2,128,1024]{2,1,0:T(8,128)(2,1)}, bf16[2,128,1024]{2,1,0:T(8,128)(2,1)}, u32[]{:S(2)}, u32[]{:S(2)}) collective-permute-start(bf16[2,128,1024]{2,1,0:T(8,128)(2,1)} %get-tuple-element.35.refs_0_), channel_id=1, source_target_pairs={{0,2},{1,3},{2,0},{3,1},{4,6},{5,7},{6,4},{7,5},{8,10},{9,11},{10,... | collective-permute-start | bytes 1572872 | tf_op jit(solution)/shard_map/ppermute | solution.py:176
  258.8 3.7 %pick_blocks.1 = (bf16[2,1024,128]{2,1,0:T(8,128)(2,1)S(1)}, bf16[2,1024,128]{2,1,0:T(8,128)(2,1)}) custom-call(s32[1]{0:T(128)} %bitcast.me, s32[16,1]{1,0:T(8,128)S(1)} %copy.14.member, s32[4]{0:T(128)S(1)} %copy-done.42, bf16[2,1280,128]{2,1,0:T(8,128)(2,1)S(1)} %split_pairs.3.refs_0_.refs_3_, ...), custom_call_target="tpu_custom_call" | custom-call | flops 1024 | bytes 1024 | tf_op jit(solution)/shard_map/pick_blocks/pallas_call | solution.py:738
  262.8 2.7 decode.1.refs_0_
  266.9 6.6 %collective-permute-done.22.came = bf16[2,2,128,1024]{3,2,1,0:T(8,128)(2,1)} collective-permute-done((bf16[2,2,128,1024]{3,2,1,0:T(8,128)(2,1)}, bf16[2,2,128,1024]{3,2,1,0:T(8,128)(2,1)}, u32[]{:S(2)}, u32[]{:S(2)}) %collective-permute-start.22) | collective-permute-done | bytes 1048608 | tf_op jit(solution)/shard_map/ppermute | solution.py:176
  273.4 3.2 %merge.3 = (f32[2,128,1024]{2,1,0:T(8,128)}, bf16[2,128,1024]{2,1,0:T(8,128)(2,1)}) custom-call(s32[1]{0:T(128)} %bitcast.1.offset, bf16[2,128,1024]{2,1,0:T(8,128)(2,1)} %copy-done.31, bf16[2,128,1024]{2,1,0:T(8,128)(2,1)} %collective-permute-done.18.across, bf16[2,128,1024]{2,1,0:T(8,128)(2,1)} %collective-permute-done.19.beside, ...), custom_call_target="tpu_custom_call" | custom-call | flops 1024 | bytes 1024 | tf_op jit(solution)/shard_map/merge/pallas_call | solution.py:613
  276.7 4.1 %collective-permute-start.23 = (bf16[2,128,1024]{2,1,0:T(8,128)(2,1)}, bf16[2,128,1024]{2,1,0:T(8,128)(2,1)S(1)}, u32[]{:S(2)}, u32[]{:S(2)}) collective-permute-start(bf16[2,128,1024]{2,1,0:T(8,128)(2,1)} %get-tuple-element.38), channel_id=1, source_target_pairs={{0,2},{1,3},{2,0},{3,1},{4,6},{5,7},{6,4},{7,5},{8,10},{9,11},{10,... | collective-permute-start | bytes 1572872 | tf_op jit(solution)/shard_map/ppermute | solution.py:176
  287.7 5.5 %collective-permute-done.23.came = bf16[2,128,1024]{2,1,0:T(8,128)(2,1)S(1)} collective-permute-done((bf16[2,128,1024]{2,1,0:T(8,128)(2,1)}, bf16[2,128,1024]{2,1,0:T(8,128)(2,1)S(1)}, u32[]{:S(2)}, u32[]{:S(2)}) %collective-permute-start.23) | collective-permute-done | bytes 524320 | tf_op jit(solution)/shard_map/ppermute | solution.py:176
  (144 shorter events, 66.5 us)
Async XLA Ops:
  0.6 122.7 %collective-permute-start.11 = (bf16[2048,1024]{1,0:T(8,128)(2,1)}, bf16[2048,1024]{1,0:T(8,128)(2,1)}, u32[]{:S(2)}, u32[]{:S(2)}) collective-permute-start(bf16[2048,1024]{1,0:T(8,128)(2,1)} %refs_1_.3), channel_id=1, source_target_pairs={{0,4},{4,0},{8,12},{12,8},{16,20},{20,16},{24,28},{28,24},{1,5},{5... | collective-permute-start | bytes 12582920 | tf_op jit(solution)/shard_map/ppermute | solution.py:176
  6.3 16.4 %collective-permute-start.2 = (bf16[2,1280,128]{2,1,0:T(8,128)(2,1)S(1)}, bf16[2,1280,128]{2,1,0:T(8,128)(2,1)S(1)}, u32[]{:S(2)}, u32[]{:S(2)}) collective-permute-start(bf16[2,1280,128]{2,1,0:T(8,128)(2,1)S(1)} %split_pairs.2.refs_0_), channel_id=1, source_target_pairs={{0,16},{4,20},{8,24},{12,28},{16,0},{20,4},{24,8},{28,12},{1,17},{... | collective-permute-start | bytes 1966088 | tf_op jit(solution)/shard_map/ppermute | solution.py:176
  10.6 16.1 %collective-permute-start.4 = (bf16[2,1280,128]{2,1,0:T(8,128)(2,1)S(1)}, bf16[2,1280,128]{2,1,0:T(8,128)(2,1)S(1)}, u32[]{:S(2)}, u32[]{:S(2)}) collective-permute-start(bf16[2,1280,128]{2,1,0:T(8,128)(2,1)S(1)} %split_pairs.3.refs_0_.refs_3_), channel_id=1, source_target_pairs={{0,8},{4,12},{8,0},{12,4},{16,24},{20,28},{24,16},{28,20},{1,9},{5... | collective-permute-start | bytes 1966088 | tf_op jit(solution)/shard_map/ppermute | solution.py:176
  22.7 18.0 %collective-permute-start.6 = (bf16[2,1280,128]{2,1,0:T(8,128)(2,1)S(1)}, bf16[2,1280,128]{2,1,0:T(8,128)(2,1)S(1)}, u32[]{:S(2)}, u32[]{:S(2)}) collective-permute-start(bf16[2,1280,128]{2,1,0:T(8,128)(2,1)S(1)} %collective-permute-done.2.refs_2_.refs_7_.refs_4_), channel_id=1, source_target_pairs={{0,8},{4,12},{8,0},{12,4},{16,24},{20,28},{24,16},{28,20},{1,9},{5... | collective-permute-start | bytes 1966088 | tf_op jit(solution)/shard_map/ppermute | solution.py:176
  22.9 20.5 %collective-permute-start.1 = (bf16[2,1280,128]{2,1,0:T(8,128)(2,1)S(1)}, bf16[2,1280,128]{2,1,0:T(8,128)(2,1)S(1)}, u32[]{:S(2)}, u32[]{:S(2)}) collective-permute-start(bf16[2,1280,128]{2,1,0:T(8,128)(2,1)S(1)} %split_pairs.3.refs_0_.refs_3_), channel_id=1, source_target_pairs={{0,4},{4,0},{8,12},{12,8},{16,20},{20,16},{24,28},{28,24},{1,5},{5... | collective-permute-start | bytes 1966088 | tf_op jit(solution)/shard_map/ppermute | solution.py:176
  23.8 19.9 %collective-permute-start.3 = (bf16[2,1280,128]{2,1,0:T(8,128)(2,1)S(1)}, bf16[2,1280,128]{2,1,0:T(8,128)(2,1)S(1)}, u32[]{:S(2)}, u32[]{:S(2)}) collective-permute-start(bf16[2,1280,128]{2,1,0:T(8,128)(2,1)S(1)} %collective-permute-done.2.refs_2_.refs_7_.refs_4_), channel_id=1, source_target_pairs={{0,4},{4,0},{8,12},{12,8},{16,20},{20,16},{24,28},{28,24},{1,5},{5... | collective-permute-start | bytes 1966088 | tf_op jit(solution)/shard_map/ppermute | solution.py:176
  26.7 17.1 %collective-permute-start.5 = (bf16[2,1280,128]{2,1,0:T(8,128)(2,1)S(1)}, bf16[2,1280,128]{2,1,0:T(8,128)(2,1)S(1)}, u32[]{:S(2)}, u32[]{:S(2)}) collective-permute-start(bf16[2,1280,128]{2,1,0:T(8,128)(2,1)S(1)} %collective-permute-done.4.refs_4_.refs_5_.refs_2_), channel_id=1, source_target_pairs={{0,4},{4,0},{8,12},{12,8},{16,20},{20,16},{24,28},{28,24},{1,5},{5... | collective-permute-start | bytes 1966088 | tf_op jit(solution)/shard_map/ppermute | solution.py:176
  40.7 20.6 %collective-permute-start.7 = (bf16[2,1280,128]{2,1,0:T(8,128)(2,1)S(1)}, bf16[2,1280,128]{2,1,0:T(8,128)(2,1)S(1)}, u32[]{:S(2)}, u32[]{:S(2)}) collective-permute-start(bf16[2,1280,128]{2,1,0:T(8,128)(2,1)S(1)} %collective-permute-done.6.refs_9_.refs_6_), channel_id=1, source_target_pairs={{0,4},{4,0},{8,12},{12,8},{16,20},{20,16},{24,28},{28,24},{1,5},{5... | collective-permute-start | bytes 1966088 | tf_op jit(solution)/shard_map/ppermute | solution.py:176
  43.4 17.8 %collective-permute-start = (bf16[4,512,128]{2,1,0:T(8,128)(2,1)S(1)}, bf16[4,512,128]{2,1,0:T(8,128)(2,1)S(1)}, u32[]{:S(2)}, u32[]{:S(2)}) collective-permute-start(bf16[4,512,128]{2,1,0:T(8,128)(2,1)S(1)} %get-tuple-element.23), channel_id=1, source_target_pairs={{0,16},{4,20},{8,24},{12,28},{16,0},{20,4},{24,8},{28,12},{1,17},{... | collective-permute-start | bytes 1572872 | tf_op jit(solution)/shard_map/ppermute | solution.py:176
  90.5 32.8 %collective-permute-start.8 = (bf16[2,128,1024]{2,1,0:T(8,128)(2,1)}, bf16[2,128,1024]{2,1,0:T(8,128)(2,1)}, u32[]{:S(2)}, u32[]{:S(2)}) collective-permute-start(bf16[2,128,1024]{2,1,0:T(8,128)(2,1)} %chunk_attention.5.refs_11_.own), channel_id=1, source_target_pairs={{0,16},{4,20},{8,24},{12,28},{16,0},{20,4},{24,8},{28,12},{1,17},{... | collective-permute-start | bytes 1572872 | tf_op jit(solution)/shard_map/ppermute | solution.py:176
  91.8 31.5 %collective-permute-start.9 = (bf16[2,128,1024]{2,1,0:T(8,128)(2,1)}, bf16[2,128,1024]{2,1,0:T(8,128)(2,1)}, u32[]{:S(2)}, u32[]{:S(2)}) collective-permute-start(bf16[2,128,1024]{2,1,0:T(8,128)(2,1)} %chunk_attention.5.refs_11_.own), channel_id=1, source_target_pairs={{0,8},{4,12},{8,0},{12,4},{16,24},{20,28},{24,16},{28,20},{1,9},{5... | collective-permute-start | bytes 1572872 | tf_op jit(solution)/shard_map/ppermute | solution.py:176
  92.1 31.2 %collective-permute-start.10 = (bf16[2,128,1024]{2,1,0:T(8,128)(2,1)}, bf16[2,128,1024]{2,1,0:T(8,128)(2,1)}, u32[]{:S(2)}, u32[]{:S(2)}) collective-permute-start(bf16[2,128,1024]{2,1,0:T(8,128)(2,1)} %chunk_attention.5.refs_11_.own), channel_id=1, source_target_pairs={{0,24},{4,28},{8,16},{12,20},{16,8},{20,12},{24,0},{28,4},{1,25},{... | collective-permute-start | bytes 1572872 | tf_op jit(solution)/shard_map/ppermute | solution.py:176
  132.1 27.7 %collective-permute-start.15 = (bf16[2,128,1024]{2,1,0:T(8,128)(2,1)}, bf16[2,128,1024]{2,1,0:T(8,128)(2,1)}, u32[]{:S(2)}, u32[]{:S(2)}) collective-permute-start(bf16[2,128,1024]{2,1,0:T(8,128)(2,1)} %get-tuple-element.28), channel_id=1, source_target_pairs={{0,8},{4,12},{8,0},{12,4},{16,24},{20,28},{24,16},{28,20},{1,9},{5... | collective-permute-start | bytes 1572872 | tf_op jit(solution)/shard_map/ppermute | solution.py:176
  132.2 28.7 %collective-permute-start.16 = (bf16[2,128,1024]{2,1,0:T(8,128)(2,1)}, bf16[2,128,1024]{2,1,0:T(8,128)(2,1)}, u32[]{:S(2)}, u32[]{:S(2)}) collective-permute-start(bf16[2,128,1024]{2,1,0:T(8,128)(2,1)} %get-tuple-element.29), channel_id=1, source_target_pairs={{0,16},{4,20},{8,24},{12,28},{16,0},{20,4},{24,8},{28,12},{1,17},{... | collective-permute-start | bytes 1572872 | tf_op jit(solution)/shard_map/ppermute | solution.py:176
  133.6 27.3 %collective-permute-start.17 = (bf16[2,128,1024]{2,1,0:T(8,128)(2,1)}, bf16[2,128,1024]{2,1,0:T(8,128)(2,1)}, u32[]{:S(2)}, u32[]{:S(2)}) collective-permute-start(bf16[2,128,1024]{2,1,0:T(8,128)(2,1)} %get-tuple-element.30), channel_id=1, source_target_pairs={{0,24},{4,28},{8,16},{12,20},{16,8},{20,12},{24,0},{28,4},{1,25},{... | collective-permute-start | bytes 1572872 | tf_op jit(solution)/shard_map/ppermute | solution.py:176
  158.2 43.3 %collective-permute-start.12 = (bf16[2,128,1024]{2,1,0:T(8,128)(2,1)}, bf16[2,128,1024]{2,1,0:T(8,128)(2,1)}, u32[]{:S(2)}, u32[]{:S(2)}) collective-permute-start(bf16[2,128,1024]{2,1,0:T(8,128)(2,1)} %chunk_attention.7.refs_0_.own), channel_id=1, source_target_pairs={{0,16},{4,20},{8,24},{12,28},{16,0},{20,4},{24,8},{28,12},{1,17},{... | collective-permute-start | bytes 1572872 | tf_op jit(solution)/shard_map/ppermute | solution.py:176
  159.5 42.0 %collective-permute-start.13 = (bf16[2,128,1024]{2,1,0:T(8,128)(2,1)}, bf16[2,128,1024]{2,1,0:T(8,128)(2,1)}, u32[]{:S(2)}, u32[]{:S(2)}) collective-permute-start(bf16[2,128,1024]{2,1,0:T(8,128)(2,1)} %chunk_attention.7.refs_0_.own), channel_id=1, source_target_pairs={{0,8},{4,12},{8,0},{12,4},{16,24},{20,28},{24,16},{28,20},{1,9},{5... | collective-permute-start | bytes 1572872 | tf_op jit(solution)/shard_map/ppermute | solution.py:176
  159.8 41.7 %collective-permute-start.14 = (bf16[2,128,1024]{2,1,0:T(8,128)(2,1)}, bf16[2,128,1024]{2,1,0:T(8,128)(2,1)}, u32[]{:S(2)}, u32[]{:S(2)}) collective-permute-start(bf16[2,128,1024]{2,1,0:T(8,128)(2,1)} %chunk_attention.7.refs_0_.own), channel_id=1, source_target_pairs={{0,24},{4,28},{8,16},{12,20},{16,8},{20,12},{24,0},{28,4},{1,25},{... | collective-permute-start | bytes 1572872 | tf_op jit(solution)/shard_map/ppermute | solution.py:176
  163.5 52.8 %collective-permute-start.21 = (bf16[2,2,128,1024]{3,2,1,0:T(8,128)(2,1)}, bf16[2,2,128,1024]{3,2,1,0:T(8,128)(2,1)}, u32[]{:S(2)}, u32[]{:S(2)}) collective-permute-start(bf16[2,2,128,1024]{3,2,1,0:T(8,128)(2,1)} %away.2.refs_4_), channel_id=1, source_target_pairs={{0,1},{1,0},{2,3},{3,2},{4,5},{5,4},{6,7},{7,6},{8,9},{9,8},{10,11... | collective-permute-start | bytes 3145736 | tf_op jit(solution)/shard_map/ppermute | solution.py:176
  231.9 41.6 %collective-permute-start.22 = (bf16[2,2,128,1024]{3,2,1,0:T(8,128)(2,1)}, bf16[2,2,128,1024]{3,2,1,0:T(8,128)(2,1)}, u32[]{:S(2)}, u32[]{:S(2)}) collective-permute-start(bf16[2,2,128,1024]{3,2,1,0:T(8,128)(2,1)} %away.3.refs_8_), channel_id=1, source_target_pairs={{0,1},{1,0},{2,3},{3,2},{4,5},{5,4},{6,7},{7,6},{8,9},{9,8},{10,11... | collective-permute-start | bytes 3145736 | tf_op jit(solution)/shard_map/ppermute | solution.py:176
  249.8 32.4 %collective-permute-start.24 = (bf16[2,128,1024]{2,1,0:T(8,128)(2,1)}, bf16[2,128,1024]{2,1,0:T(8,128)(2,1)}, u32[]{:S(2)}, u32[]{:S(2)}) collective-permute-start(bf16[2,128,1024]{2,1,0:T(8,128)(2,1)} %get-tuple-element.35.refs_0_), channel_id=1, source_target_pairs={{0,2},{1,3},{2,0},{3,1},{4,6},{5,7},{6,4},{7,5},{8,10},{9,11},{10,... | collective-permute-start | bytes 1572872 | tf_op jit(solution)/shard_map/ppermute | solution.py:176
  262.5 21.9 %collective-permute-start.25 = (bf16[2,1024,128]{2,1,0:T(8,128)(2,1)}, bf16[2,1024,128]{2,1,0:T(8,128)(2,1)}, u32[]{:S(2)}, u32[]{:S(2)}) collective-permute-start(bf16[2,1024,128]{2,1,0:T(8,128)(2,1)} %get-tuple-element.40), channel_id=1, source_target_pairs={{0,16},{4,20},{8,24},{12,28},{16,0},{20,4},{24,8},{28,12},{1,17},{... | collective-permute-start | bytes 1572872 | tf_op jit(solution)/shard_map/ppermute | solution.py:176
  265.6 15.2 %collective-permute-start.26 = (bf16[16,128]{1,0:T(8,128)(2,1)S(1)}, bf16[16,128]{1,0:T(8,128)(2,1)S(1)}, u32[]{:S(2)}, u32[]{:S(2)}) collective-permute-start(bf16[16,128]{1,0:T(8,128)(2,1)S(1)} %decode.1.refs_0_), channel_id=1, source_target_pairs={{0,16},{4,20},{8,24},{12,28},{16,0},{20,4},{24,8},{28,12},{1,17},{... | collective-permute-start | bytes 12296 | tf_op jit(solution)/shard_map/ppermute | solution.py:176
  276.7 16.5 %collective-permute-start.23 = (bf16[2,128,1024]{2,1,0:T(8,128)(2,1)}, bf16[2,128,1024]{2,1,0:T(8,128)(2,1)S(1)}, u32[]{:S(2)}, u32[]{:S(2)}) collective-permute-start(bf16[2,128,1024]{2,1,0:T(8,128)(2,1)} %get-tuple-element.38), channel_id=1, source_target_pairs={{0,2},{1,3},{2,0},{3,1},{4,6},{5,7},{6,4},{7,5},{8,10},{9,11},{10,... | collective-permute-start | bytes 1572872 | tf_op jit(solution)/shard_map/ppermute | solution.py:176
  (48 other events, 464.8 us)
